TPU v7x, 512 devices: a whole 4x8x8 slice. The times are simulated.
512 devices in a mesh: cfg: 2 (over core), seq: 128 (over y_lo, z, x), tile: 2 (over y_hi).
Axes of the slice: x: 4, y: 8 (y_hi: 2, y_lo: 4; y = y_hi * 4 + y_lo), z: 8, core: 2. Of those that a mesh axis runs over, the one named last changes fastest.
Arguments:
- section_input: bfloat16 [4, 128, 1024, 384], P('tile', None, 'seq'), may hold values from -6 to 6
- norm_gain: float32 [384], replicated, may hold values from 0.5 to 1.5
- conv_weight: bfloat16 [384, 864], replicated, may hold values from -0.0625 to 0.0625
- conv_bias: float32 [32], replicated, may hold values from -3 to 3
- mean_weight: float32 [32, 16], replicated, may hold values from -1 to 1
- mean_bias: float32 [16], replicated, may hold values from -3 to 3
- noisy_tokens: bfloat16 [131072, 64], P(('seq', 'tile')), may hold values from -6 to 6
- mask_tokens: bfloat16 [131072, 128], P(('seq', 'tile')), may hold values from 0 to 1
- patch_weight: bfloat16 [64, 5120], replicated, may hold values from -0.75 to 0.75
- patch_bias: float32 [5120], replicated, may hold values from -3 to 3
- context_weight: bfloat16 [192, 5120], replicated, may hold values from -0.4375 to 0.4375
- context_bias: float32 [5120], replicated, may hold values from -3 to 3
- norm_shift: float32 [5120], replicated, may hold values from -3 to 3
- norm_scale: float32 [5120], replicated, may hold values from -3 to 3
Outputs:
- block_input: bfloat16 [131072, 5120], P(('seq', 'tile'))
All inputs are finite; a program needn't handle non-finite values.
Results may differ from a plain program's by a relative error of at most 0.004.
Values may be sent and summed in bfloat16 or wider, within the bound.
No kernel may reach another device: no remote copies, remote signals or barrier semaphores. Data moves between devices by JAX's collectives and lax.ppermute only.
A program may use at most 128 MiB of HBM per device.

v0:
```python
import jax
import jax.numpy as jnp
from jax import lax
from jax.sharding import PartitionSpec as P

K = 3


def with_halo(x, sides, width):
    for axis, dim in sides:
        size, length = (lax.axis_size(axis), x.shape[dim])
        up = [(i, (i + 1) % size) for i in range(size - 1)]
        down = [(j, i) for i, j in up]
        last = lax.slice_in_dim(x, length - width, length, axis=dim)
        first = lax.slice_in_dim(x, 0, width, axis=dim)
        before = lax.ppermute(last, axis, up)
        after = lax.ppermute(first, axis, down)
        x = jnp.concatenate([before, x, after], axis=dim)
    return x


def from_behind(x, axis, by):
    length = lax.axis_size(axis)
    pairs = [(i, i + by) for i in range(length) if 0 <= i + by < length]
    return lax.ppermute(x, axis, pairs)


def from_everyone(x, axis):
    length = lax.axis_size(axis)
    return lax.all_to_all(jnp.broadcast_to(x[None], (length, *x.shape)), axis, 0, 0, tiled=True)


def joined_along(parts, dim):
    lengths = list(parts.shape[1:])
    lengths[dim] *= parts.shape[0]
    return jnp.moveaxis(parts, 0, dim).reshape(lengths)


def collect(x, axis, dim):
    parts = from_everyone(x, axis)
    return joined_along(parts, dim)


def body(
    section_input,
    norm_gain,
    conv_weight,
    conv_bias,
    mean_weight,
    mean_bias,
    noisy_tokens,
    mask_tokens,
    patch_weight,
    patch_bias,
    context_weight,
    context_bias,
    norm_shift,
    norm_scale,
):
    frames, height, columns, channels = section_input.shape
    values = section_input.astype(jnp.float32)
    energy = jnp.mean(values * values, axis=-1, keepdims=True)
    activation = jax.nn.silu(values * lax.rsqrt(energy + 1e-06) * norm_gain).astype(jnp.bfloat16)
    kernel = conv_weight.reshape(channels, K * K * K, -1)
    out_chans = kernel.shape[-1]
    tap_matrix = kernel.reshape(channels, K * K * K * out_chans)
    spread = jnp.dot(
        activation.reshape(-1, channels), tap_matrix, preferred_element_type=jnp.float32
    )
    spread = spread.reshape(frames, height, columns, K * K * K, out_chans)
    extended = jnp.zeros((frames + 2, height + 2, columns + 2, out_chans), jnp.float32)
    for step_t in range(K):
        for step_h in range(K):
            for step_w in range(K):
                tap_index = (step_t * K + step_h) * K + step_w
                pad_plan = (
                    (2 - step_t, step_t),
                    (2 - step_h, step_h),
                    (2 - step_w, step_w),
                    (0, 0),
                )
                extended = extended + jnp.pad(spread[:, :, :, tap_index], pad_plan)
    extended = extended[:, 1 : height + 1]
    spill_edges = jnp.stack([extended[:, :, 0], extended[:, :, columns + 1]], 2)
    spill_edges = with_halo(spill_edges.astype(jnp.bfloat16), (("seq", 2),), 1).astype(
        spill_edges.dtype
    )
    interior = extended[:, :, 1 : columns + 1]
    interior = interior.at[:, :, 0].add(spill_edges[:, :, 0])
    interior = interior.at[:, :, columns - 1].add(spill_edges[:, :, 3])
    carried = from_behind(interior[frames:].astype(jnp.bfloat16), "tile", 1).astype(jnp.float32)
    convolved = interior[:frames].at[:2].add(carried)
    convolved = convolved + conv_bias
    partial_value = jnp.dot(
        convolved.reshape(-1, out_chans), mean_weight, precision=lax.Precision.HIGHEST
    )
    latent = (partial_value + mean_bias).astype(jnp.bfloat16)
    latent_dim = latent.shape[-1]
    latent = latent.reshape(frames, height // 2, 2, columns // 2, 2, latent_dim)
    patches = latent.transpose(0, 1, 3, 5, 2, 4).reshape(
        frames * (height // 2), columns // 2 * 4 * latent_dim
    )
    row_width = patches.shape[1]
    seq_count = lax.axis_size("seq")
    tile_count = lax.axis_size("tile")
    gathered = collect(patches, "tile", 0)
    grouped = gathered.reshape(seq_count, tile_count, -1, row_width)
    own_part = lax.dynamic_index_in_dim(grouped, lax.axis_index("tile"), 1, keepdims=False)
    arrived = lax.all_to_all(own_part, "seq", split_axis=0, concat_axis=0, tiled=True)
    arrived = arrived.reshape(seq_count, -1, columns // 2, 4 * latent_dim)
    latent_tokens = arrived.transpose(1, 0, 2, 3).reshape(-1, 4 * latent_dim)
    split_at = 4 * latent_dim
    main_part = jnp.dot(noisy_tokens, patch_weight, preferred_element_type=jnp.float32) + patch_bias
    context_part = jnp.dot(
        latent_tokens, context_weight[:split_at], preferred_element_type=jnp.float32
    )
    context_part = (
        context_part
        + jnp.dot(mask_tokens, context_weight[split_at:], preferred_element_type=jnp.float32)
        + context_bias
    )
    combined = main_part + context_part
    centred = combined - jnp.mean(combined, axis=-1, keepdims=True)
    variance = jnp.mean(centred * centred, axis=-1, keepdims=True)
    return (centred * lax.rsqrt(variance + 1e-06) * (1.0 + norm_scale) + norm_shift).astype(
        jnp.bfloat16
    )


def solution(mesh):
    placed = (
        P("tile", None, "seq", None),
        P(),
        P(),
        P(),
        P(),
        P(),
        P(("seq", "tile"), None),
        P(("seq", "tile"), None),
        P(),
        P(),
        P(),
        P(),
        P(),
        P(),
    )
    return jax.shard_map(
        body, mesh=mesh, in_specs=placed, out_specs=P(("seq", "tile"), None), check_vma=False
    )
```

profile of v0, /device:TPU:2, one launch (start us, length us, event | category | flops | bytes accessed | tf_op | source)
XLA Modules:
  0.0 104.8 jit_solution(9694567645515674341)
XLA Ops:
  0.0 0.0 copy-start
  0.0 1.9 %fusion = f32[2,128,8]{2,1,0:T(8,128)S(1)} fusion(bf16[2,128,8,384]{3,2,1,0:T(8,128)(2,1)} %param.22), kind=kLoop, calls=%fused_computation.5 | loop fusion | flops 2357248 | bytes 1581056 | tf_op jit(solution)/shard_map/reduce_sum | solution.py:62
  2.0 0.1 copy.169
  2.0 0.1 copy.170
  2.2 0.0 copy-done.1
  2.2 0.0 copy-done.11
  2.2 1.0 fusion.9
  3.2 0.0 copy-done
  3.2 2.0 %fusion.10 = f32[2,128,8,27,32]{1,4,3,2,0:T(8,128)S(1)} fusion(bf16[27,32,384,1,1]{2,1,0,4,3:T(8,128)(2,1)S(1)} %bitcast.130, bf16[2,128,8,384,1]{3,2,1,0,4:T(8,128)(2,1)S(1)} %fusion.9), kind=kOutput, calls=%fused_computation.16 | convolution fusion | flops 1358954496 | bytes 9314304 | tf_op jit(solution)/shard_map/dot_general | solution.py:67
  5.2 0.8 slice_bitcast_fusion.26
  6.0 0.2 slice_bitcast_fusion.25
  6.2 3.5 %fusion.18 = (bf16[4,130,10,32]{1,3,2,0:T(8,128)(2,1)S(1)}, f32[4,130,10,32]{1,3,2,0:T(8,128)S(1)}) fusion(f32[2,128,8,32]{1,3,2,0:T(8,128)S(1)} %get-tuple-element.76, f32[2,128,8,32]{1,3,2,0:T(8,128)S(1)} %get-tuple-element.77, f32[2,128,8,32]{1,3,2,0:T(8,128)S(1)} %get-tuple-element.52, f32[2,128,8,32]{1,3,2,0:T(8,128)S(1)} %get-tuple-element.53, ...), kind=kLoop, calls=%fused_computation.64 | loop fusion | flops 4492800 | bytes 8076288 | tf_op jit(solution)/shard_map/convert.3
  9.7 0.0 copy-start.13
  9.7 0.1 fusion.19
  9.8 3.4 %collective-permute-start = (bf16[4,128,1,32]{1,3,2,0:T(8,128)(2,1)S(1)}, bf16[4,128,1,32]{1,3,2,0:T(8,128)(2,1)S(1)}, u32[]{:S(2)}, u32[]{:S(2)}) collective-permute-start(bf16[4,128,1,32]{1,3,2,0:T(8,128)(2,1)S(1)} %get-tuple-element.78), channel_id=1, source_target_pairs={{0,2},{2,4},{4,6},{6,8},{8,10},{10,12},{12,14},{14,16},{16,18},{18... | collective-permute-start | bytes 98312 | tf_op jit(solution)/shard_map/ppermute | solution.py:16
  13.2 5.7 %collective-permute-start.1 = (bf16[4,128,1,32]{1,3,2,0:T(8,128)(2,1)S(1)}, bf16[4,128,1,32]{1,3,2,0:T(8,128)(2,1)S(1)}, u32[]{:S(2)}, u32[]{:S(2)}) collective-permute-start(bf16[4,128,1,32]{1,3,2,0:T(8,128)(2,1)S(1)} %get-tuple-element.79), channel_id=1, source_target_pairs={{2,0},{4,2},{6,4},{8,6},{10,8},{12,10},{14,12},{16,14},{18,16},{20... | collective-permute-start | bytes 98312 | tf_op jit(solution)/shard_map/ppermute | solution.py:17
  18.9 0.2 slice.261
  19.1 0.0 copy-start.10
  19.1 0.0 copy-start.12
  19.1 0.0 collective-permute-done
  19.1 1.3 %collective-permute-done.1 = bf16[4,128,1,32]{1,3,2,0:T(8,128)(2,1)S(1)} collective-permute-done((bf16[4,128,1,32]{1,3,2,0:T(8,128)(2,1)S(1)}, bf16[4,128,1,32]{1,3,2,0:T(8,128)(2,1)S(1)}, u32[]{:S(2)}, u32[]{:S(2)}) %collective-permute-start.1) | collective-permute-done | bytes 32800 | tf_op jit(solution)/shard_map/ppermute | solution.py:17
  20.5 0.1 fusion.17
  20.6 6.3 %collective-permute-start.2 = (bf16[2,128,8,32]{1,3,2,0:T(8,128)(2,1)S(1)}, bf16[2,128,8,32]{1,3,2,0:T(8,128)(2,1)S(1)}, u32[]{:S(2)}, u32[]{:S(2)}) collective-permute-start(bf16[2,128,8,32]{1,3,2,0:T(8,128)(2,1)S(1)} %slice.307), channel_id=1, source_target_pairs={{0,1},{2,3},{4,5},{6,7},{8,9},{10,11},{12,13},{14,15},{16,17},{18,... | collective-permute-start | bytes 393224 | tf_op jit(solution)/shard_map/ppermute | solution.py:25
  26.9 2.5 %collective-permute-done.2 = bf16[2,128,8,32]{1,3,2,0:T(8,128)(2,1)S(1)} collective-permute-done((bf16[2,128,8,32]{1,3,2,0:T(8,128)(2,1)S(1)}, bf16[2,128,8,32]{1,3,2,0:T(8,128)(2,1)S(1)}, u32[]{:S(2)}, u32[]{:S(2)}) %collective-permute-start.2) | collective-permute-done | bytes 131104 | tf_op jit(solution)/shard_map/ppermute | solution.py:25
  29.3 0.0 copy-done.13
  29.4 0.1 fusion.15
  29.4 0.4 copy.198
  29.8 0.0 copy-done.10
  29.9 0.0 copy-done.12
  29.9 0.0 copy-start.3
  29.9 0.0 copy-start.5
  29.9 1.0 fusion.8
  30.9 0.3 copy.199
  31.2 0.6 copy.200
  31.8 0.1 broadcast_in_dim.4
  31.9 0.1 copy.201
  32.0 0.7 broadcast_in_dim.5
  32.7 7.7 %all-to-all-start = ((bf16[2,128,256]{2,1,0:T(8,128)(2,1)}), bf16[2,128,256]{2,1,0:T(8,128)(2,1)S(1)}, u32[]{:S(2)}, u32[]{:S(2)}) async-start(bf16[2,128,256]{2,1,0:T(8,128)(2,1)} %broadcast_in_dim.5), calls=%async_computation | async-start | bytes 262144 | tf_op jit(solution)/shard_map/all_to_all | solution.py:30
  40.4 0.0 copy-done.3
  40.4 0.0 copy-done.5
  40.4 5.4 %fusion.21 = f32[512,5120]{1,0:T(8,128)} fusion(bf16[512,64]{0,1:T(8,128)(2,1)S(1)} %copy-done.5, bf16[64,5120]{1,0:T(8,128)(2,1)S(1)} %copy-done.3), kind=kOutput, calls=%fused_computation.67 | convolution fusion | flops 335544320 | bytes 11206656 | tf_op jit(solution)/shard_map/dot_general | solution.py:113
  45.8 3.1 %all-to-all-done = bf16[2,128,256]{2,1,0:T(8,128)(2,1)S(1)} async-done(((bf16[2,128,256]{2,1,0:T(8,128)(2,1)}), bf16[2,128,256]{2,1,0:T(8,128)(2,1)S(1)}, u32[]{:S(2)}, u32[]{:S(2)}) %all-to-all-start) | async-done | bytes 131104 | tf_op jit(solution)/shard_map/all_to_all | solution.py:30
  48.9 0.1 reshape_reshape.3
  48.9 0.1 dynamic-slice_bitcast_fusion
  49.1 0.5 broadcast.177
  49.6 1.0 reduce.7
  50.6 0.7 reshape.149
  51.3 19.8 %all-to-all-start.1 = ((bf16[128,2,128]{2,1,0:T(2,128)(2,1)}), bf16[128,2,128]{2,1,0:T(2,128)(2,1)S(1)}, u32[]{:S(2)}, u32[]{:S(2)}) async-start(bf16[128,2,128]{2,1,0:T(2,128)(2,1)} %reshape.149), calls=%async_computation.1 | async-start | bytes 131072 | tf_op jit(solution)/shard_map/all_to_all | solution.py:109
  71.1 0.0 copy-done.9
  71.1 11.6 %all-to-all-done.1 = bf16[128,2,128]{2,1,0:T(2,128)(2,1)S(1)} async-done(((bf16[128,2,128]{2,1,0:T(2,128)(2,1)}), bf16[128,2,128]{2,1,0:T(2,128)(2,1)S(1)}, u32[]{:S(2)}, u32[]{:S(2)}) %all-to-all-start.1) | async-done | bytes 65568 | tf_op jit(solution)/shard_map/all_to_all | solution.py:109
  82.8 0.4 reduce.6
  83.2 0.1 reshape_transpose_reshape.3
  83.3 0.0 copy-start.2
  83.3 0.0 copy-start.4
  83.3 0.0 copy-start.6
  83.3 0.0 copy-start.7
  83.4 6.7 %fusion.13 = f32[512,5120]{1,0:T(8,128)} fusion(bf16[512,64]{1,0:T(8,128)(2,1)S(1)} %reshape_transpose_reshape.3, bf16[192,5120]{1,0:T(8,128)(2,1)} %param.32), kind=kOutput, calls=%fused_computation.20 | convolution fusion | flops 335544320 | bytes 11206656 | tf_op jit(solution)/shard_map/dot_general | solution.py:114
  90.1 0.0 copy-done.2
  90.1 0.0 copy-done.4
  90.1 0.0 copy-done.6
  90.1 8.4 %fusion.20 = (f32[512]{0:T(512)S(1)}, f32[512,5120]{1,0:T(8,128)S(1)}) fusion(f32[5120]{0:T(1024)S(1)} %copy-done.6, f32[512,5120]{1,0:T(8,128)} %fusion.13, bf16[512,128]{1,0:T(8,128)(2,1)S(1)} %copy-done.4, bf16[192,5120]{1,0:T(8,128)(2,1)S(1)} %copy-done.2, f32[512,5120]{1,0:T(8,128)} %fusion.21, f32[5120]{0:T(1024)S(1)} %copy-done.7), kind=kOutput, calls=%fused_computation.66 | convolution fusion | flops 684195328 | bytes 32942080 | tf_op jit(solution)/shard_map/dot_general | solution.py:119
  98.5 0.0 copy-start.8
  98.5 1.2 %multiply_reduce_fusion = f32[512]{0:T(512)S(1)} fusion(f32[512,5120]{1,0:T(8,128)S(1)} %get-tuple-element.81, f32[512]{0:T(512)S(1)} %broadcast_multiply_fusion), kind=kLoop, calls=%fused_computation.1 | loop fusion | flops 7863808 | bytes 10489856 | tf_op jit(solution)/shard_map/reduce_sum | solution.py:124
  99.7 5.1 %add_convert_fusion = bf16[512,5120]{1,0:T(8,128)(2,1)} fusion(f32[512,5120]{1,0:T(8,128)S(1)} %get-tuple-element.81, f32[5120]{0:T(1024)S(1)} %copy-done.8, f32[5120]{0:T(1024)S(1)} %broadcast_add_fusion, f32[512]{0:T(512)S(1)} %add_rsqrt_fusion.1, f32[512]{0:T(512)S(1)} %broadcast_multiply_fusion), kind=kLoop, calls=%fused_computation | loop fusion | flops 13107200 | bytes 15773696 | tf_op jit(solution)/shard_map/convert_element_type | solution.py:125
  (12 shorter events, 0.1 us)
Async XLA Ops:
  0.0 3.2 %copy-start = (bf16[384,864]{0,1:T(8,128)(2,1)S(1)}, bf16[384,864]{0,1:T(8,128)(2,1)}, u32[]{:S(2)}) copy-start(bf16[384,864]{0,1:T(8,128)(2,1)} %param.24) | copy-start | bytes 1990660
  0.0 2.2 %copy-start.1 = (bf16[2,128,8,384]{3,2,1,0:T(8,128)(2,1)S(1)}, bf16[2,128,8,384]{3,2,1,0:T(8,128)(2,1)}, u32[]{:S(2)}) copy-start(bf16[2,128,8,384]{3,2,1,0:T(8,128)(2,1)} %param.22) | copy-start | bytes 4718596
  0.0 2.2 %copy-start.11 = (f32[384]{0:T(512)S(1)}, f32[384]{0:T(512)}, u32[]{:S(2)}) copy-start(f32[384]{0:T(512)} %param.23) | copy-start | bytes 4612
  9.7 19.7 %copy-start.13 = (f32[32]{0:T(128)S(1)}, f32[32]{0:T(128)}, u32[]{:S(2)}) copy-start(f32[32]{0:T(128)} %param.25) | copy-start | bytes 388
  9.8 9.3 %collective-permute-start = (bf16[4,128,1,32]{1,3,2,0:T(8,128)(2,1)S(1)}, bf16[4,128,1,32]{1,3,2,0:T(8,128)(2,1)S(1)}, u32[]{:S(2)}, u32[]{:S(2)}) collective-permute-start(bf16[4,128,1,32]{1,3,2,0:T(8,128)(2,1)S(1)} %get-tuple-element.78), channel_id=1, source_target_pairs={{0,2},{2,4},{4,6},{6,8},{8,10},{10,12},{12,14},{14,16},{16,18},{18... | collective-permute-start | bytes 98312 | tf_op jit(solution)/shard_map/ppermute | solution.py:16
  13.2 7.3 %collective-permute-start.1 = (bf16[4,128,1,32]{1,3,2,0:T(8,128)(2,1)S(1)}, bf16[4,128,1,32]{1,3,2,0:T(8,128)(2,1)S(1)}, u32[]{:S(2)}, u32[]{:S(2)}) collective-permute-start(bf16[4,128,1,32]{1,3,2,0:T(8,128)(2,1)S(1)} %get-tuple-element.79), channel_id=1, source_target_pairs={{2,0},{4,2},{6,4},{8,6},{10,8},{12,10},{14,12},{16,14},{18,16},{20... | collective-permute-start | bytes 98312 | tf_op jit(solution)/shard_map/ppermute | solution.py:17
  19.1 10.8 %copy-start.10 = (f32[32,16]{0,1:T(8,128)S(1)}, f32[32,16]{0,1:T(8,128)}, u32[]{:S(2)}) copy-start(f32[32,16]{0,1:T(8,128)} %param.26) | copy-start | bytes 6148
  19.1 10.8 %copy-start.12 = (f32[16]{0:T(128)S(1)}, f32[16]{0:T(128)}, u32[]{:S(2)}) copy-start(f32[16]{0:T(128)} %param.27) | copy-start | bytes 196
  20.6 8.8 %collective-permute-start.2 = (bf16[2,128,8,32]{1,3,2,0:T(8,128)(2,1)S(1)}, bf16[2,128,8,32]{1,3,2,0:T(8,128)(2,1)S(1)}, u32[]{:S(2)}, u32[]{:S(2)}) collective-permute-start(bf16[2,128,8,32]{1,3,2,0:T(8,128)(2,1)S(1)} %slice.307), channel_id=1, source_target_pairs={{0,1},{2,3},{4,5},{6,7},{8,9},{10,11},{12,13},{14,15},{16,17},{18,... | collective-permute-start | bytes 393224 | tf_op jit(solution)/shard_map/ppermute | solution.py:25
  29.9 10.6 %copy-start.3 = (bf16[64,5120]{1,0:T(8,128)(2,1)S(1)}, bf16[64,5120]{1,0:T(8,128)(2,1)}, u32[]{:S(2)}) copy-start(bf16[64,5120]{1,0:T(8,128)(2,1)} %param.30) | copy-start | bytes 1966084
  29.9 10.5 %copy-start.5 = (bf16[512,64]{0,1:T(8,128)(2,1)S(1)}, bf16[512,64]{0,1:T(8,128)(2,1)}, u32[]{:S(2)}) copy-start(bf16[512,64]{0,1:T(8,128)(2,1)} %param.28) | copy-start | bytes 196612
  32.7 16.2 %all-to-all-start = ((bf16[2,128,256]{2,1,0:T(8,128)(2,1)}), bf16[2,128,256]{2,1,0:T(8,128)(2,1)S(1)}, u32[]{:S(2)}, u32[]{:S(2)}) async-start(bf16[2,128,256]{2,1,0:T(8,128)(2,1)} %broadcast_in_dim.5), calls=%async_computation | async-start | bytes 262144 | tf_op jit(solution)/shard_map/all_to_all | solution.py:30
  40.4 30.7 %copy-start.9 = (f32[5120]{0:T(1024)S(1)}, f32[5120]{0:T(1024)}, u32[]{:S(2)}) copy-start(f32[5120]{0:T(1024)} %param.35) | copy-start | bytes 61444
  51.3 31.5 %all-to-all-start.1 = ((bf16[128,2,128]{2,1,0:T(2,128)(2,1)}), bf16[128,2,128]{2,1,0:T(2,128)(2,1)S(1)}, u32[]{:S(2)}, u32[]{:S(2)}) async-start(bf16[128,2,128]{2,1,0:T(2,128)(2,1)} %reshape.149), calls=%async_computation.1 | async-start | bytes 131072 | tf_op jit(solution)/shard_map/all_to_all | solution.py:109
  83.3 6.8 %copy-start.2 = (bf16[192,5120]{1,0:T(8,128)(2,1)S(1)}, bf16[192,5120]{1,0:T(8,128)(2,1)}, u32[]{:S(2)}) copy-start(bf16[192,5120]{1,0:T(8,128)(2,1)} %param.32) | copy-start | bytes 5898244
  83.3 6.8 %copy-start.4 = (bf16[512,128]{1,0:T(8,128)(2,1)S(1)}, bf16[512,128]{1,0:T(8,128)(2,1)}, u32[]{:S(2)}) copy-start(bf16[512,128]{1,0:T(8,128)(2,1)} %param.29) | copy-start | bytes 393220
  83.3 6.7 %copy-start.6 = (f32[5120]{0:T(1024)S(1)}, f32[5120]{0:T(1024)}, u32[]{:S(2)}) copy-start(f32[5120]{0:T(1024)} %param.33) | copy-start | bytes 61444
  83.3 6.7 %copy-start.7 = (f32[5120]{0:T(1024)S(1)}, f32[5120]{0:T(1024)}, u32[]{:S(2)}) copy-start(f32[5120]{0:T(1024)} %param.31) | copy-start | bytes 61444
  98.5 1.2 %copy-start.8 = (f32[5120]{0:T(1024)S(1)}, f32[5120]{0:T(1024)}, u32[]{:S(2)}) copy-start(f32[5120]{0:T(1024)} %param.34) | copy-start | bytes 61444
where the time goes:
time: 105 us
  starting transfers between devices  42.9 us (41%)
  matrix products  23.6 us (22%)
  waiting for transfers between devices  18.5 us (18%)
  other arithmetic  14.2 us (14%)
  local copies, waits for them, and re-layouts  5.2 us (5%)
    all_to_all x1, starting transfers between devices, body(): lax.all_to_all(own_part, 'seq', split_axis=0, concat_axis=0, tiled=True)  19.8 us
    all_to_all x1, waiting for transfers between devices, body(): lax.all_to_all(own_part, 'seq', split_axis=0, concat_axis=0, tiled=True)  11.6 us
    dot_general x1, matrix products, body(): jnp.dot(mask_tokens, context_weight[split_at:], preferred_element_type=jn...  8.42 us
    all_to_all x1, starting transfers between devices, from_everyone(): lax.all_to_all(jnp.broadcast_to(x[None], (length, *x.shape)), axis, 0, 0,...  7.72 us
    dot_general x1, matrix products, body(): jnp.dot(latent_tokens, context_weight[:split_at], preferred_element_type=...  6.72 us
    ppermute x1, starting transfers between devices, from_behind(): return lax.ppermute(x, axis, pairs)  6.25 us
    ppermute x1, starting transfers between devices, with_halo(): after = lax.ppermute(first, axis, down)  5.7 us
    dot_general x1, matrix products, body(): jnp.dot(noisy_tokens, patch_weight, preferred_element_type=jnp.float32)  5.38 us
  transfers between devices with their start and end apart: 5, of which 4 were waited for; matrix products, arithmetic and copies ran while one was open for 5% of the time, Pallas kernels for 0%

commit v1 on v0

v1 whole, which is shorter than its diff:
```python
import jax
import jax.numpy as jnp
from jax import lax
from jax.experimental import pallas as pl
from jax.experimental.pallas import tpu as pltpu
from jax.sharding import PartitionSpec as P

BF = jnp.bfloat16
F32 = jnp.float32
NT = (((1,), (1,)), ((), ()))


def iota(shape, dim):
    return lax.broadcasted_iota(jnp.int32, shape, dim)


def dot(a, b):
    return jnp.dot(a, b, preferred_element_type=F32)


def dot_nt(a, b):
    return lax.dot_general(a, b, NT, preferred_element_type=F32)


def halves(x):
    high = x.astype(BF)
    return high, (x - high.astype(F32)).astype(BF)


SLOTS = ((0, 2), (0, 1), (1, 2), (1, 1), (0, 0), (0, 2), (1, 0), (1, 2))


def encode_kernel(tile_ref, x_ref, gain_ref, wt_ref, mwt_ref, out_ref, act, big, parts):
    frames, height, columns, channels = x_ref.shape
    pairs = height // 2
    rows = frames * columns
    z, o = mwt_ref.shape
    taps = wt_ref.shape[0] // o
    pick = (iota((o, taps * o), 1) % o == iota((o, taps * o), 0)).astype(BF)
    own = iota((taps * z, taps * o), 0) // z == iota((taps * z, taps * o), 1) // o
    folded = None
    for part in halves(mwt_ref[...]):
        spread = dot(part, pick)
        block = jnp.where(own, jnp.concatenate([spread] * taps, 0), 0.0).astype(BF)
        term = dot(block, wt_ref[...])
        folded = term if folded is None else folded + term
    folded = folded.astype(BF)
    nothing = jnp.zeros((z, channels), BF)
    for t in range(3):
        for slot, (a, e) in enumerate(SLOTS):
            at = (t * 8 + slot) * z
            for k in range(4):
                b = k - a
                tap = ((t * 3 + b) * 3 + e) * z
                value = folded[tap : tap + z] if 0 <= b < 3 else nothing
                big[at : at + z, k * channels : (k + 1) * channels] = value

    zero = jnp.zeros((rows, channels), BF)
    act[0, :, :channels] = zero
    act[pairs, :, channels:] = zero
    step = 8
    gain = gain_ref[...].reshape(1, 1, 1, channels)

    @pl.loop(0, pairs // step)
    def _(j):
        x = x_ref[:, pl.ds(j * 2 * step, 2 * step)].astype(F32)
        energy = jnp.mean(x * x, axis=-1, keepdims=True)
        v = x * lax.rsqrt(energy + 1e-6) * gain
        v = v * (0.5 + 0.5 * jnp.tanh(0.5 * v))
        v = jnp.concatenate([v[f] for f in range(frames)], axis=1).astype(BF)
        v = v.reshape(step, 2, rows, channels)
        act[pl.ds(j * step, step), :, channels:] = v[:, 0]
        act[pl.ds(j * step + 1, step), :, :channels] = v[:, 1]

    first = tile_ref[0] == 0
    lanes = 8 * z
    chunk = 16
    for c in range(pairs // chunk):
        low = act[c * chunk : (c + 1) * chunk].reshape(chunk * rows, 2 * channels)
        high = act[c * chunk + 1 : (c + 1) * chunk + 1].reshape(chunk * rows, 2 * channels)
        out = dot_nt(low, big[:, : 2 * channels]) + dot_nt(high, big[:, 2 * channels :])
        out = out.reshape(chunk // 2, 2, frames, columns, 3 * lanes)
        part = lambda p, f, t: out[:, p, f, :, t * lanes : (t + 1) * lanes]
        for p in range(2):
            ext = (
                part(p, 0, 2),
                part(p, 0, 1) + part(p, 1, 2),
                part(p, 0, 0) + part(p, 1, 1),
                part(p, 1, 0),
            )
            slots = (
                jnp.where(first, ext[0], 0.0),
                jnp.where(first, ext[1], 0.0),
                jnp.where(first, ext[2], ext[0]),
                jnp.where(first, ext[3], ext[1]),
            )
            for f in range(4):
                at = ((p * 4 + f) * (pairs // 2) + c * chunk // 2) * columns
                size = chunk // 2 * columns
                parts[at : at + size] = slots[f].reshape(size, lanes)

    total = parts.shape[0]
    even = parts[pl.ds(0, total // 2, stride=2)]
    odd = parts[pl.ds(1, total // 2, stride=2)]
    slot = iota((1, lanes), 1) // z
    near = pltpu.roll(even, lanes - z, 1)
    far = pltpu.roll(even, lanes - 3 * z, 1)
    moved = jnp.where((slot == 0) | (slot == 2), near, jnp.where((slot == 1) | (slot == 3), far, 0.0))
    back = (slot == 5) | (slot == 7)
    out_ref[...] = jnp.where(back, even, moved + odd).astype(BF)


def prep_kernel(
    ctx_ref, patch_ref, pb_ref, cb_ref, shift_ref, scale_ref, noisy_ref, mask_ref, conv_bias_ref, mwt_ref, mb_ref,
    w_ref, vec_ref, gram_ref, aux_ref, base_ref,
):
    lat = 4 * mwt_ref.shape[0]
    z = lat // 4
    width = ctx_ref.shape[1]
    row, col = iota((lat, lat), 0), iota((lat, lat), 1)
    order = (col == (row % z) * 4 + row // z).astype(BF)
    w_ref[:lat] = dot(order, ctx_ref[:lat]).astype(BF)
    w_ref[lat : 2 * lat] = patch_ref[...]
    w_ref[2 * lat :] = ctx_ref[lat:]
    bias = pb_ref[...] + cb_ref[...]
    mean_b = jnp.mean(bias, axis=1, keepdims=True)
    centred = bias - mean_b
    vec_ref[0:1] = bias
    vec_ref[1:2] = 1.0 + scale_ref[...]
    vec_ref[2:3] = shift_ref[...]
    vec_ref[3:8] = jnp.zeros((5, width), F32)
    w = w_ref[...]
    high, low = halves(centred)
    rows = jnp.concatenate([jnp.ones((1, width), BF), high, low, jnp.zeros((5, width), BF)], 0)
    sums = dot_nt(rows, w)
    mean_w = sums[0:1] / width
    ones = jnp.ones((128, width), BF)
    mean_col = dot_nt(w, ones)[:, :1] / width
    gram = dot_nt(w, w) / width - mean_col * mean_w
    high, low = halves(gram)
    gram_ref[:, : gram.shape[1]] = high
    gram_ref[:, gram.shape[1] :] = low
    size = w.shape[0]
    square = jnp.mean(centred * centred, axis=1, keepdims=True)
    tiled = jnp.concatenate([mwt_ref[...]] * 8, 0)
    conv_bias = jnp.broadcast_to(conv_bias_ref[...], (8, conv_bias_ref.shape[1]))
    latent_bias = lax.dot_general(conv_bias, tiled, NT, precision=lax.Precision.HIGHEST, preferred_element_type=F32)
    latent_bias = latent_bias[:1] + jnp.concatenate([mb_ref[...]] * 8, 1)
    aux_ref[0:1] = mean_w
    aux_ref[1:2] = 2.0 * (sums[1:2] + sums[2:3]) / width
    aux_ref[2:3] = jnp.broadcast_to(mean_b, (1, size))
    aux_ref[3:4] = jnp.broadcast_to(square, (1, size))
    aux_ref[4:5] = jnp.concatenate([latent_bias] * (size // latent_bias.shape[1]), 1)
    aux_ref[5:8] = jnp.zeros((3, size), F32)
    place = (iota((lat, 2 * lat), 1) == iota((lat, 2 * lat), 0) + lat).astype(BF)
    noisy = lax.dot_general(noisy_ref[...], place, (((0,), (0,)), ((), ())), preferred_element_type=F32)
    base_ref[:, : 2 * lat] = noisy.astype(BF)
    base_ref[:, 2 * lat :] = mask_ref[...]


def embed_kernel(arrived_ref, base_ref, w_ref, vec_ref, gram_ref, aux_ref, out_ref, lhs, inv, off):
    @pl.when(pl.program_id(0) == 0)
    def _():
        tokens = base_ref.shape[0]
        lanes = arrived_ref.shape[1]
        z = lanes // 8
        both = arrived_ref[:tokens].astype(F32) + arrived_ref[tokens:].astype(F32)
        crossed = pltpu.roll(both, lanes // 2, 1)
        row = iota((tokens, 1), 0)
        down = jnp.where(row == 0, 0.0, pltpu.roll(crossed, 1, 0))
        up = jnp.where(row == tokens - 1, 0.0, pltpu.roll(crossed, tokens - 1, 0))
        lane = iota((1, lanes), 1)
        latent = both + jnp.where(lane // z % 2 == 0, down, up) + aux_ref[4:5, :lanes]
        front = jnp.where(lane < lanes // 2, latent, base_ref[:, :lanes].astype(F32))
        x = jnp.concatenate([front.astype(BF), base_ref[:, lanes:]], 1)
        lhs[...] = x
        size = x.shape[1]
        y = dot(x, gram_ref[:, :size]) + dot(x, gram_ref[:, size:])
        xf = x.astype(F32)
        mean = jnp.sum(xf * aux_ref[0:1], axis=1, keepdims=True) + aux_ref[2:3, :128]
        variance = jnp.sum((y + aux_ref[1:2]) * xf, axis=1, keepdims=True) + aux_ref[3:4, :128]
        scale = lax.rsqrt(jnp.maximum(variance, 0.0) + 1e-6)
        inv[...] = scale
        off[...] = mean * scale

    combined = dot(lhs[...], w_ref[...]) + vec_ref[0:1]
    copies = combined.shape[1] // inv.shape[1]
    scale = jnp.concatenate([inv[...]] * copies, 1)
    offset = jnp.concatenate([off[...]] * copies, 1)
    out_ref[...] = ((combined * scale - offset) * vec_ref[1:2] + vec_ref[2:3]).astype(BF)


def body(
    section_input, norm_gain, conv_weight, conv_bias, mean_weight, mean_bias, noisy_tokens, mask_tokens,
    patch_weight, patch_bias, context_weight, context_bias, norm_shift, norm_scale,
):
    frames, height, columns, channels = section_input.shape
    z = mean_weight.shape[1]
    tokens = noisy_tokens.shape[0]
    width = patch_weight.shape[1]
    features = patch_weight.shape[0] + context_weight.shape[0]
    shards = lax.axis_size("tile") * lax.axis_size("seq")
    tile = lax.axis_index("tile").astype(jnp.int32).reshape(1)
    vmem = pl.BlockSpec(memory_space=pltpu.VMEM)
    params = pltpu.CompilerParams(vmem_limit_bytes=48 * 1024 * 1024)
    row = lambda v: v.reshape(1, -1)
    message = pl.pallas_call(
        encode_kernel,
        out_shape=jax.ShapeDtypeStruct((shards * 4, 8 * z), BF),
        in_specs=[pl.BlockSpec(memory_space=pltpu.SMEM)] + [vmem] * 4,
        out_specs=vmem,
        scratch_shapes=[
            pltpu.VMEM((height // 2 + 1, frames * columns, 2 * channels), BF),
            pltpu.VMEM((3 * 8 * z, 4 * channels), BF),
            pltpu.VMEM((shards * 8, 8 * z), F32),
        ],
        compiler_params=params,
        name="encode",
    )(tile, section_input, row(norm_gain), conv_weight.T, mean_weight.T)
    arrived = lax.all_to_all(message.reshape(shards, 4, 8 * z), ("tile", "seq"), 0, 0)
    arrived = arrived.reshape(shards * 4, 8 * z)
    weights, vectors, gram, aux, base = pl.pallas_call(
        prep_kernel,
        out_shape=(
            jax.ShapeDtypeStruct((features, width), BF),
            jax.ShapeDtypeStruct((8, width), F32),
            jax.ShapeDtypeStruct((features, 2 * features), BF),
            jax.ShapeDtypeStruct((8, features), F32),
            jax.ShapeDtypeStruct((tokens, features), BF),
        ),
        in_specs=[vmem] * 11,
        out_specs=(vmem,) * 5,
        compiler_params=params,
        cost_estimate=pl.CostEstimate(flops=2 * features * features * width, bytes_accessed=6_000_000, transcendentals=0),
        name="prep",
    )(
        context_weight, patch_weight, row(patch_bias), row(context_bias), row(norm_shift), row(norm_scale),
        noisy_tokens.T, mask_tokens, row(conv_bias), mean_weight.T, row(mean_bias),
    )
    block = 1024
    return pl.pallas_call(
        embed_kernel,
        grid=(width // block,),
        out_shape=jax.ShapeDtypeStruct((tokens, width), BF),
        in_specs=[
            vmem,
            vmem,
            pl.BlockSpec((features, block), lambda n: (0, n)),
            pl.BlockSpec((8, block), lambda n: (0, n)),
            vmem,
            vmem,
        ],
        out_specs=pl.BlockSpec((tokens, block), lambda n: (0, n)),
        scratch_shapes=[
            pltpu.VMEM((tokens, features), BF),
            pltpu.VMEM((tokens, 128), F32),
            pltpu.VMEM((tokens, 128), F32),
        ],
        compiler_params=params,
        name="embed",
    )(arrived, base, weights, vectors, gram, aux)


def solution(mesh):
    placed = (
        P("tile", None, "seq", None),
        P(),
        P(),
        P(),
        P(),
        P(),
        P(("seq", "tile"), None),
        P(("seq", "tile"), None),
        P(),
        P(),
        P(),
        P(),
        P(),
        P(),
    )
    return jax.shard_map(
        body, mesh=mesh, in_specs=placed, out_specs=P(("seq", "tile"), None), check_vma=False
    )
```

time: 105 us -> 55 us (0.52)
  the two profiles are of different devices: /device:TPU:2 before, /device:TPU:8 now
where the time goes in v1:
time: 55 us; the launch traced here: 54.4 us
  starting transfers between devices  21.4 us (39%)
  Pallas kernels  14.3 us (26%)
  local copies, waits for them, and re-layouts  12.4 us (23%)
  waiting for transfers between devices  6.2 us (11%)
    all_to_all x1, starting transfers between devices, body(): lax.all_to_all(message.reshape(shards, 4, 8 * z), ('tile', 'seq'), 0, 0)  21.4 us
    unnamed x34, local copies, waits for them, and re-layouts  11.6 us
    all_to_all x1, waiting for transfers between devices, body(): lax.all_to_all(message.reshape(shards, 4, 8 * z), ('tile', 'seq'), 0, 0)  6.2 us
    pallas_call x1, Pallas kernels, body(): pl.pallas_call(encode_kernel, out_shape=jax.ShapeDtypeStruct((shards * 4,...  5.49 us
    pallas_call x1, Pallas kernels, body(): pl.pallas_call(embed_kernel, grid=(width // block,), out_shape=jax.ShapeD...  5.18 us
    pallas_call x1, Pallas kernels, body(): pl.pallas_call(prep_kernel, out_shape=(jax.ShapeDtypeStruct((features, wi...  3.6 us
  transfers between devices with their start and end apart: 1, of which 1 were waited for; matrix products, arithmetic and copies ran while one was open for 0% of the time, Pallas kernels for 7%

profile of v1, /device:TPU:8, one launch (start us, length us, event | category | flops | bytes accessed | tf_op | source)
XLA Modules:
  0.0 54.4 jit_solution(1913514407058067465)
XLA Ops:
  0.0 0.0 copy-start.1
  0.0 0.8 %reshape.31.gain_ref = f32[1,384]{1,0:T(1,128)S(1)} reshape(f32[384]{0:T(512)} %param.15) | data formatting | bytes 3072 | tf_op jit(solution)/shard_map/reshape | solution.py:206
  0.8 0.0 copy-start.2
  0.8 1.4 %copy-done.2 = bf16[2,128,8,384]{3,2,1,0:T(8,128)(2,1)S(1)} copy-done((bf16[2,128,8,384]{3,2,1,0:T(8,128)(2,1)S(1)}, bf16[2,128,8,384]{3,2,1,0:T(8,128)(2,1)}, u32[]{:S(2)}) %copy-start.2) | copy-done | bytes 1572888
  2.2 0.0 copy-start.3
  2.2 1.1 %copy-done.3 = bf16[384,864]{0,1:T(8,128)(2,1)S(1)} copy-done((bf16[384,864]{0,1:T(8,128)(2,1)S(1)}, bf16[384,864]{0,1:T(8,128)(2,1)}, u32[]{:S(2)}) %copy-start.3) | copy-done | bytes 663576
  3.3 0.0 copy-start.9
  3.3 0.7 %copy-done.9 = f32[32,16]{0,1:T(8,128)S(1)} copy-done((f32[32,16]{0,1:T(8,128)S(1)}, f32[32,16]{0,1:T(8,128)}, u32[]{:S(2)}) %copy-start.9) | copy-done | bytes 2072
  4.0 0.0 copy-start.4
  4.0 0.0 copy-start.7
  4.0 0.0 copy-start.10
  4.0 5.5 %encode.1 = bf16[1024,128]{1,0:T(8,128)(2,1)} custom-call(s32[1]{0:T(128)} %bitcast.tile_ref, bf16[2,128,8,384]{3,2,1,0:T(8,128)(2,1)S(1)} %copy-done.2, f32[1,384]{1,0:T(1,128)S(1)} %reshape.31.gain_ref, bf16[864,384]{1,0:T(8,128)(2,1)S(1)} %bitcast.13, f32[16,32]{1,0:T(8,128)S(1)} %bitcast.15), custom_call_target="tpu_custom_call" | custom-call | tf_op jit(solution)/shard_map/encode/pallas_call | solution.py:207
  9.5 21.4 %all-to-all-start = ((bf16[256,4,128]{2,1,0:T(4,128)(2,1)}), bf16[256,4,128]{2,1,0:T(4,128)(2,1)S(1)}, u32[]{:S(2)}, u32[]{:S(2)}) async-start(bf16[256,4,128]{2,1,0:T(4,128)(2,1)} %bitcast.3), calls=%async_computation | async-start | bytes 524288 | tf_op jit(solution)/shard_map/all_to_all | solution.py:220
  31.0 0.0 copy-done.1
  31.0 0.0 copy-done.4
  31.0 0.0 copy-done.7
  31.0 0.0 copy-done.10
  31.0 0.0 copy-start.8
  31.0 0.8 %copy-done.8 = bf16[512,64]{0,1:T(8,128)(2,1)S(1)} copy-done((bf16[512,64]{0,1:T(8,128)(2,1)S(1)}, bf16[512,64]{0,1:T(8,128)(2,1)}, u32[]{:S(2)}) %copy-start.8) | copy-done | bytes 65560
  31.8 0.0 copy-start.11
  31.8 0.7 %copy-done.11 = f32[5120]{0:T(1024)S(1)} copy-done((f32[5120]{0:T(1024)S(1)}, f32[5120]{0:T(1024)}, u32[]{:S(2)}) %copy-start.11) | copy-done | bytes 20504
  32.6 0.0 copy-start.12
  32.6 0.7 %copy-done.12 = f32[5120]{0:T(1024)S(1)} copy-done((f32[5120]{0:T(1024)S(1)}, f32[5120]{0:T(1024)}, u32[]{:S(2)}) %copy-start.12) | copy-done | bytes 20504
  33.3 0.0 copy-start.13
  33.3 0.7 %copy-done.13 = f32[5120]{0:T(1024)S(1)} copy-done((f32[5120]{0:T(1024)S(1)}, f32[5120]{0:T(1024)}, u32[]{:S(2)}) %copy-start.13) | copy-done | bytes 20504
  34.0 0.0 copy-start.14
  34.0 0.7 %copy-done.14 = f32[5120]{0:T(1024)S(1)} copy-done((f32[5120]{0:T(1024)S(1)}, f32[5120]{0:T(1024)}, u32[]{:S(2)}) %copy-start.14) | copy-done | bytes 20504
  34.7 0.0 copy-start.15
  34.8 0.7 %copy-done.15 = f32[32]{0:T(128)S(1)} copy-done((f32[32]{0:T(128)S(1)}, f32[32]{0:T(128)}, u32[]{:S(2)}) %copy-start.15) | copy-done | bytes 152
  35.4 0.0 copy-start.16
  35.4 0.7 %copy-done.16 = f32[16]{0:T(128)S(1)} copy-done((f32[16]{0:T(128)S(1)}, f32[16]{0:T(128)}, u32[]{:S(2)}) %copy-start.16) | copy-done | bytes 88
  36.1 3.6 %prep.1 = (bf16[256,5120]{1,0:T(8,128)(2,1)}, f32[8,5120]{1,0:T(8,128)S(1)}, bf16[256,512]{1,0:T(8,128)(2,1)S(1)}, f32[8,256]{1,0:T(8,128)S(1)}, bf16[512,256]{1,0:T(8,128)(2,1)S(1)}) custom-call(bf16[192,5120]{1,0:T(8,128)(2,1)S(1)} %copy-done.1, bf16[64,5120]{1,0:T(8,128)(2,1)S(1)} %copy-done.4, f32[1,5120]{1,0:T(1,128)S(1)} %bitcast.17, ...), custom_call_target="tpu_custom_call" | custom-call | flops 671088640 | bytes 6000000 | tf_op jit(solution)/shard_map/prep/pallas_call | solution.py:222
  39.7 0.0 copy-start.5
  39.7 0.7 %copy-done.5 = f32[8,5120]{1,0:T(8,128)} copy-done((f32[8,5120]{1,0:T(8,128)}, f32[8,5120]{1,0:T(8,128)S(1)}, u32[]{:S(2)}) %copy-start.5) | copy-done | bytes 163864
  40.3 6.2 %all-to-all-done = bf16[256,4,128]{2,1,0:T(4,128)(2,1)S(1)} async-done(((bf16[256,4,128]{2,1,0:T(4,128)(2,1)}), bf16[256,4,128]{2,1,0:T(4,128)(2,1)S(1)}, u32[]{:S(2)}, u32[]{:S(2)}) %all-to-all-start) | async-done | bytes 262176 | tf_op jit(solution)/shard_map/all_to_all | solution.py:220
  46.5 0.0 copy-start
  46.5 1.7 %copy-done = bf16[256,5120]{1,0:T(8,128)(2,1)S(1)} copy-done((bf16[256,5120]{1,0:T(8,128)(2,1)S(1)}, bf16[256,5120]{1,0:T(8,128)(2,1)}, u32[]{:S(2)}) %copy-start) | copy-done | bytes 2621464
  48.3 0.0 copy-start.6
  48.3 0.9 %copy-done.6 = f32[8,5120]{1,0:T(8,128)S(1)} copy-done((f32[8,5120]{1,0:T(8,128)S(1)}, f32[8,5120]{1,0:T(8,128)}, u32[]{:S(2)}) %copy-start.6) | copy-done | bytes 163864
  49.2 5.2 %embed.1 = bf16[512,5120]{1,0:T(8,128)(2,1)} custom-call(bf16[1024,128]{1,0:T(8,128)(2,1)S(1)} %bitcast.12, bf16[512,256]{1,0:T(8,128)(2,1)S(1)} %get-tuple-element.10.base_ref, bf16[256,5120]{1,0:T(8,128)(2,1)S(1)} %copy-done, f32[8,5120]{1,0:T(8,128)S(1)} %copy-done.6, bf16[256,512]{1,0:T(8,128)(2,1)S(1)} %get-tuple-element.13.gram_ref, ...), custom_call_target="tpu_custom_call" | custom-call | tf_op jit(solution)/shard_map/embed/pallas_call | solution.py:241
Async XLA Ops:
  0.0 31.0 %copy-start.1 = (bf16[192,5120]{1,0:T(8,128)(2,1)S(1)}, bf16[192,5120]{1,0:T(8,128)(2,1)}, u32[]{:S(2)}) copy-start(bf16[192,5120]{1,0:T(8,128)(2,1)} %ctx_ref.1) | copy-start | bytes 5898244
  0.8 1.4 %copy-start.2 = (bf16[2,128,8,384]{3,2,1,0:T(8,128)(2,1)S(1)}, bf16[2,128,8,384]{3,2,1,0:T(8,128)(2,1)}, u32[]{:S(2)}) copy-start(bf16[2,128,8,384]{3,2,1,0:T(8,128)(2,1)} %x_ref.1) | copy-start | bytes 4718596
  2.2 1.1 %copy-start.3 = (bf16[384,864]{0,1:T(8,128)(2,1)S(1)}, bf16[384,864]{0,1:T(8,128)(2,1)}, u32[]{:S(2)}) copy-start(bf16[384,864]{0,1:T(8,128)(2,1)} %param.16) | copy-start | bytes 1990660
  3.3 0.7 %copy-start.9 = (f32[32,16]{0,1:T(8,128)S(1)}, f32[32,16]{0,1:T(8,128)}, u32[]{:S(2)}) copy-start(f32[32,16]{0,1:T(8,128)} %param.18) | copy-start | bytes 6148
  4.0 26.9 %copy-start.4 = (bf16[64,5120]{1,0:T(8,128)(2,1)S(1)}, bf16[64,5120]{1,0:T(8,128)(2,1)}, u32[]{:S(2)}) copy-start(bf16[64,5120]{1,0:T(8,128)(2,1)} %patch_ref.1) | copy-start | bytes 1966084
  4.0 27.0 %copy-start.7 = (bf16[512,128]{1,0:T(8,128)(2,1)S(1)}, bf16[512,128]{1,0:T(8,128)(2,1)}, u32[]{:S(2)}) copy-start(bf16[512,128]{1,0:T(8,128)(2,1)} %mask_ref.1) | copy-start | bytes 393220
  4.0 27.0 %copy-start.10 = (f32[32,16]{0,1:T(8,128)S(1)}, f32[32,16]{0,1:T(8,128)}, u32[]{:S(2)}) copy-start(f32[32,16]{0,1:T(8,128)} %param.18) | copy-start | bytes 6148
  9.5 37.0 %all-to-all-start = ((bf16[256,4,128]{2,1,0:T(4,128)(2,1)}), bf16[256,4,128]{2,1,0:T(4,128)(2,1)S(1)}, u32[]{:S(2)}, u32[]{:S(2)}) async-start(bf16[256,4,128]{2,1,0:T(4,128)(2,1)} %bitcast.3), calls=%async_computation | async-start | bytes 524288 | tf_op jit(solution)/shard_map/all_to_all | solution.py:220
  31.0 0.8 %copy-start.8 = (bf16[512,64]{0,1:T(8,128)(2,1)S(1)}, bf16[512,64]{0,1:T(8,128)(2,1)}, u32[]{:S(2)}) copy-start(bf16[512,64]{0,1:T(8,128)(2,1)} %param.20) | copy-start | bytes 196612
  31.8 0.7 %copy-start.11 = (f32[5120]{0:T(1024)S(1)}, f32[5120]{0:T(1024)}, u32[]{:S(2)}) copy-start(f32[5120]{0:T(1024)} %param.23) | copy-start | bytes 61444
  32.6 0.7 %copy-start.12 = (f32[5120]{0:T(1024)S(1)}, f32[5120]{0:T(1024)}, u32[]{:S(2)}) copy-start(f32[5120]{0:T(1024)} %param.25) | copy-start | bytes 61444
  33.3 0.7 %copy-start.13 = (f32[5120]{0:T(1024)S(1)}, f32[5120]{0:T(1024)}, u32[]{:S(2)}) copy-start(f32[5120]{0:T(1024)} %param.26) | copy-start | bytes 61444
  34.0 0.7 %copy-start.14 = (f32[5120]{0:T(1024)S(1)}, f32[5120]{0:T(1024)}, u32[]{:S(2)}) copy-start(f32[5120]{0:T(1024)} %param.27) | copy-start | bytes 61444
  34.7 0.7 %copy-start.15 = (f32[32]{0:T(128)S(1)}, f32[32]{0:T(128)}, u32[]{:S(2)}) copy-start(f32[32]{0:T(128)} %param.17) | copy-start | bytes 388
  35.4 0.7 %copy-start.16 = (f32[16]{0:T(128)S(1)}, f32[16]{0:T(128)}, u32[]{:S(2)}) copy-start(f32[16]{0:T(128)} %param.19) | copy-start | bytes 196
  39.7 0.7 %copy-start.5 = (f32[8,5120]{1,0:T(8,128)}, f32[8,5120]{1,0:T(8,128)S(1)}, u32[]{:S(2)}) copy-start(f32[8,5120]{1,0:T(8,128)S(1)} %get-tuple-element.12.vec_ref) | copy-start | bytes 491524
  46.5 1.7 %copy-start = (bf16[256,5120]{1,0:T(8,128)(2,1)S(1)}, bf16[256,5120]{1,0:T(8,128)(2,1)}, u32[]{:S(2)}) copy-start(bf16[256,5120]{1,0:T(8,128)(2,1)} %get-tuple-element.11.w_ref) | copy-start | bytes 7864324
  48.3 0.9 %copy-start.6 = (f32[8,5120]{1,0:T(8,128)S(1)}, f32[8,5120]{1,0:T(8,128)}, u32[]{:S(2)}) copy-start(f32[8,5120]{1,0:T(8,128)} %copy-done.5) | copy-start | bytes 491524

commit v2 on v1

--- a/solution.py
+++ b/solution.py
@@ -30,12 +30,39 @@
 SLOTS = ((0, 2), (0, 1), (1, 2), (1, 1), (0, 0), (0, 2), (1, 0), (1, 2))
 
 
-def encode_kernel(tile_ref, x_ref, gain_ref, wt_ref, mwt_ref, out_ref, act, big, parts):
+def in_hbm(*arrays):
+    return [pltpu.with_memory_space_constraint(x, pltpu.HBM) for x in arrays]
+
+
+def in_vmem(*arrays):
+    return [pltpu.with_memory_space_constraint(x, pltpu.VMEM) for x in arrays]
+
+
+def fetch(sem, pairs):
+    copies = [pltpu.make_async_copy(src, dst, sem.at[n]) for n, (src, dst) in enumerate(pairs)]
+    for copy in copies:
+        copy.start()
+    return copies
+
+
+STEP = 8
+
+
+def encode_kernel(tile_ref, x_hbm, gain_hbm, wt_hbm, mwt_hbm, out_ref, x_ref, gain_ref, wt_ref, mwt_ref, act, big, parts, sem):
     frames, height, columns, channels = x_ref.shape
     pairs = height // 2
     rows = frames * columns
     z, o = mwt_ref.shape
     taps = wt_ref.shape[0] // o
+    span = lambda ref, n: ref.at[:, pl.ds(n * 2 * STEP, 2 * STEP)]
+    blocks = pairs // STEP
+    copies = fetch(
+        sem,
+        [(mwt_hbm, mwt_ref), (wt_hbm, wt_ref), (gain_hbm, gain_ref)]
+        + [(span(x_hbm, n), span(x_ref, n)) for n in range(blocks)],
+    )
+    copies[0].wait()
+    copies[1].wait()
     pick = (iota((o, taps * o), 1) % o == iota((o, taps * o), 0)).astype(BF)
     own = iota((taps * z, taps * o), 0) // z == iota((taps * z, taps * o), 1) // o
     folded = None
@@ -58,11 +85,11 @@
     zero = jnp.zeros((rows, channels), BF)
     act[0, :, :channels] = zero
     act[pairs, :, channels:] = zero
-    step = 8
+    step = STEP
+    copies[2].wait()
     gain = gain_ref[...].reshape(1, 1, 1, channels)
-
-    @pl.loop(0, pairs // step)
-    def _(j):
+    for j in range(blocks):
+        copies[3 + j].wait()
         x = x_ref[:, pl.ds(j * 2 * step, 2 * step)].astype(F32)
         energy = jnp.mean(x * x, axis=-1, keepdims=True)
         v = x * lax.rsqrt(energy + 1e-6) * gain
@@ -111,23 +138,42 @@
 
 
 def prep_kernel(
-    ctx_ref, patch_ref, pb_ref, cb_ref, shift_ref, scale_ref, noisy_ref, mask_ref, conv_bias_ref, mwt_ref, mb_ref,
+    ctx_hbm, patch_hbm, pb_hbm, cb_hbm, shift_hbm, scale_hbm, noisy_hbm, mask_hbm, conv_bias_hbm, mwt_hbm, mb_hbm,
     w_ref, vec_ref, gram_ref, aux_ref, base_ref,
+    ctx_ref, rows_ref, noisy_ref, conv_bias_ref, mwt_ref, mb_ref, sem,
 ):
-    lat = 4 * mwt_ref.shape[0]
-    z = lat // 4
-    width = ctx_ref.shape[1]
+    z = mwt_ref.shape[0]
+    lat = 4 * z
+    width = w_ref.shape[1]
+    size = w_ref.shape[0]
+    copies = fetch(
+        sem,
+        [
+            (ctx_hbm.at[pl.ds(0, lat)], ctx_ref),
+            (patch_hbm, w_ref.at[pl.ds(lat, lat)]),
+            (ctx_hbm.at[pl.ds(lat, 2 * lat)], w_ref.at[pl.ds(2 * lat, 2 * lat)]),
+            (pb_hbm, rows_ref.at[0]),
+            (cb_hbm, rows_ref.at[1]),
+            (shift_hbm, rows_ref.at[2]),
+            (scale_hbm, rows_ref.at[3]),
+            (noisy_hbm, noisy_ref),
+            (mask_hbm, base_ref.at[:, pl.ds(2 * lat, 2 * lat)]),
+            (conv_bias_hbm, conv_bias_ref),
+            (mwt_hbm, mwt_ref),
+            (mb_hbm, mb_ref),
+        ],
+    )
+    for copy in copies:
+        copy.wait()
     row, col = iota((lat, lat), 0), iota((lat, lat), 1)
     order = (col == (row % z) * 4 + row // z).astype(BF)
-    w_ref[:lat] = dot(order, ctx_ref[:lat]).astype(BF)
-    w_ref[lat : 2 * lat] = patch_ref[...]
-    w_ref[2 * lat :] = ctx_ref[lat:]
-    bias = pb_ref[...] + cb_ref[...]
+    w_ref[:lat] = dot(order, ctx_ref[...]).astype(BF)
+    bias = rows_ref[0] + rows_ref[1]
     mean_b = jnp.mean(bias, axis=1, keepdims=True)
     centred = bias - mean_b
     vec_ref[0:1] = bias
-    vec_ref[1:2] = 1.0 + scale_ref[...]
-    vec_ref[2:3] = shift_ref[...]
+    vec_ref[1:2] = 1.0 + rows_ref[3]
+    vec_ref[2:3] = rows_ref[2]
     vec_ref[3:8] = jnp.zeros((5, width), F32)
     w = w_ref[...]
     high, low = halves(centred)
@@ -138,9 +184,8 @@
     mean_col = dot_nt(w, ones)[:, :1] / width
     gram = dot_nt(w, w) / width - mean_col * mean_w
     high, low = halves(gram)
-    gram_ref[:, : gram.shape[1]] = high
-    gram_ref[:, gram.shape[1] :] = low
-    size = w.shape[0]
+    gram_ref[:, :size] = high
+    gram_ref[:, size:] = low
     square = jnp.mean(centred * centred, axis=1, keepdims=True)
     tiled = jnp.concatenate([mwt_ref[...]] * 8, 0)
     conv_bias = jnp.broadcast_to(conv_bias_ref[...], (8, conv_bias_ref.shape[1]))
@@ -155,39 +200,43 @@
     place = (iota((lat, 2 * lat), 1) == iota((lat, 2 * lat), 0) + lat).astype(BF)
     noisy = lax.dot_general(noisy_ref[...], place, (((0,), (0,)), ((), ())), preferred_element_type=F32)
     base_ref[:, : 2 * lat] = noisy.astype(BF)
-    base_ref[:, 2 * lat :] = mask_ref[...]
-
-
-def embed_kernel(arrived_ref, base_ref, w_ref, vec_ref, gram_ref, aux_ref, out_ref, lhs, inv, off):
-    @pl.when(pl.program_id(0) == 0)
-    def _():
-        tokens = base_ref.shape[0]
-        lanes = arrived_ref.shape[1]
-        z = lanes // 8
-        both = arrived_ref[:tokens].astype(F32) + arrived_ref[tokens:].astype(F32)
-        crossed = pltpu.roll(both, lanes // 2, 1)
-        row = iota((tokens, 1), 0)
-        down = jnp.where(row == 0, 0.0, pltpu.roll(crossed, 1, 0))
-        up = jnp.where(row == tokens - 1, 0.0, pltpu.roll(crossed, tokens - 1, 0))
-        lane = iota((1, lanes), 1)
-        latent = both + jnp.where(lane // z % 2 == 0, down, up) + aux_ref[4:5, :lanes]
-        front = jnp.where(lane < lanes // 2, latent, base_ref[:, :lanes].astype(F32))
-        x = jnp.concatenate([front.astype(BF), base_ref[:, lanes:]], 1)
-        lhs[...] = x
-        size = x.shape[1]
-        y = dot(x, gram_ref[:, :size]) + dot(x, gram_ref[:, size:])
-        xf = x.astype(F32)
-        mean = jnp.sum(xf * aux_ref[0:1], axis=1, keepdims=True) + aux_ref[2:3, :128]
-        variance = jnp.sum((y + aux_ref[1:2]) * xf, axis=1, keepdims=True) + aux_ref[3:4, :128]
-        scale = lax.rsqrt(jnp.maximum(variance, 0.0) + 1e-6)
-        inv[...] = scale
-        off[...] = mean * scale
-
-    combined = dot(lhs[...], w_ref[...]) + vec_ref[0:1]
-    copies = combined.shape[1] // inv.shape[1]
-    scale = jnp.concatenate([inv[...]] * copies, 1)
-    offset = jnp.concatenate([off[...]] * copies, 1)
-    out_ref[...] = ((combined * scale - offset) * vec_ref[1:2] + vec_ref[2:3]).astype(BF)
+
+
+BLOCKS = 10
+
+
+def embed_kernel(arrived_ref, base_ref, w_ref, vec_ref, gram_ref, aux_ref, out_hbm, out_ref, sem):
+    block = w_ref.shape[1] // BLOCKS
+    columns = lambda n: pl.ds(n * block, block)
+    tokens = base_ref.shape[0]
+    lanes = arrived_ref.shape[1]
+    z = lanes // 8
+    both = arrived_ref[:tokens].astype(F32) + arrived_ref[tokens:].astype(F32)
+    crossed = pltpu.roll(both, lanes // 2, 1)
+    row = iota((tokens, 1), 0)
+    down = jnp.where(row == 0, 0.0, pltpu.roll(crossed, 1, 0))
+    up = jnp.where(row == tokens - 1, 0.0, pltpu.roll(crossed, tokens - 1, 0))
+    lane = iota((1, lanes), 1)
+    latent = both + jnp.where(lane // z % 2 == 0, down, up) + aux_ref[4:5, :lanes]
+    front = jnp.where(lane < lanes // 2, latent, base_ref[:, :lanes].astype(F32))
+    x = jnp.concatenate([front.astype(BF), base_ref[:, lanes:]], 1)
+    size = x.shape[1]
+    y = dot(x, gram_ref[:, :size]) + dot(x, gram_ref[:, size:])
+    xf = x.astype(F32)
+    mean = jnp.sum(xf * aux_ref[0:1], axis=1, keepdims=True) + aux_ref[2:3, :1]
+    variance = jnp.sum((y + aux_ref[1:2]) * xf, axis=1, keepdims=True) + aux_ref[3:4, :1]
+    scale = lax.rsqrt(jnp.maximum(variance, 0.0) + 1e-6)
+    offset = mean * scale
+    sent = []
+    for n in range(BLOCKS):
+        at = slice(n * block, (n + 1) * block)
+        combined = dot(x, w_ref[:, at]) + vec_ref[0:1, at]
+        out_ref[:, at] = ((combined * scale - offset) * vec_ref[1:2, at] + vec_ref[2:3, at]).astype(BF)
+        copy = pltpu.make_async_copy(out_ref.at[:, columns(n)], out_hbm.at[:, columns(n)], sem.at[n])
+        copy.start()
+        sent.append(copy)
+    for copy in sent:
+        copy.wait()
 
 
 def body(
@@ -202,21 +251,29 @@
     shards = lax.axis_size("tile") * lax.axis_size("seq")
     tile = lax.axis_index("tile").astype(jnp.int32).reshape(1)
     vmem = pl.BlockSpec(memory_space=pltpu.VMEM)
-    params = pltpu.CompilerParams(vmem_limit_bytes=48 * 1024 * 1024)
+    hbm = pl.BlockSpec(memory_space=pltpu.HBM)
+    params = lambda mib: pltpu.CompilerParams(vmem_limit_bytes=mib * 1024 * 1024)
     row = lambda v: v.reshape(1, -1)
+    taps_out = conv_weight.shape[1]
+    dma = pltpu.SemaphoreType.DMA
     message = pl.pallas_call(
         encode_kernel,
         out_shape=jax.ShapeDtypeStruct((shards * 4, 8 * z), BF),
-        in_specs=[pl.BlockSpec(memory_space=pltpu.SMEM)] + [vmem] * 4,
+        in_specs=[pl.BlockSpec(memory_space=pltpu.SMEM)] + [hbm] * 4,
         out_specs=vmem,
         scratch_shapes=[
+            pltpu.VMEM(section_input.shape, BF),
+            pltpu.VMEM(norm_gain.shape, F32),
+            pltpu.VMEM((taps_out, channels), BF),
+            pltpu.VMEM(mean_weight.shape[::-1], F32),
             pltpu.VMEM((height // 2 + 1, frames * columns, 2 * channels), BF),
             pltpu.VMEM((3 * 8 * z, 4 * channels), BF),
             pltpu.VMEM((shards * 8, 8 * z), F32),
+            dma((3 + height // 2 // STEP,)),
         ],
-        compiler_params=params,
+        compiler_params=params(24),
         name="encode",
-    )(tile, section_input, row(norm_gain), conv_weight.T, mean_weight.T)
+    )(tile, *in_hbm(section_input, norm_gain, conv_weight.T, mean_weight.T))
     arrived = lax.all_to_all(message.reshape(shards, 4, 8 * z), ("tile", "seq"), 0, 0)
     arrived = arrived.reshape(shards * 4, 8 * z)
     weights, vectors, gram, aux, base = pl.pallas_call(
@@ -228,37 +285,38 @@
             jax.ShapeDtypeStruct((8, features), F32),
             jax.ShapeDtypeStruct((tokens, features), BF),
         ),
-        in_specs=[vmem] * 11,
+        in_specs=[hbm] * 11,
         out_specs=(vmem,) * 5,
-        compiler_params=params,
+        scratch_shapes=[
+            pltpu.VMEM((4 * z, width), BF),
+            pltpu.VMEM((4, 1, width), F32),
+            pltpu.VMEM(noisy_tokens.shape[::-1], BF),
+            pltpu.VMEM((1, conv_bias.shape[0]), F32),
+            pltpu.VMEM(mean_weight.shape[::-1], F32),
+            pltpu.VMEM((1, z), F32),
+            dma((12,)),
+        ],
+        compiler_params=params(24),
         cost_estimate=pl.CostEstimate(flops=2 * features * features * width, bytes_accessed=6_000_000, transcendentals=0),
         name="prep",
     )(
-        context_weight, patch_weight, row(patch_bias), row(context_bias), row(norm_shift), row(norm_scale),
-        noisy_tokens.T, mask_tokens, row(conv_bias), mean_weight.T, row(mean_bias),
-    )
-    block = 1024
+        *in_hbm(
+            context_weight, patch_weight, row(patch_bias), row(context_bias), row(norm_shift), row(norm_scale),
+            noisy_tokens.T, mask_tokens, row(conv_bias), mean_weight.T, row(mean_bias),
+        )
+    )
     return pl.pallas_call(
         embed_kernel,
-        grid=(width // block,),
         out_shape=jax.ShapeDtypeStruct((tokens, width), BF),
-        in_specs=[
-            vmem,
-            vmem,
-            pl.BlockSpec((features, block), lambda n: (0, n)),
-            pl.BlockSpec((8, block), lambda n: (0, n)),
-            vmem,
-            vmem,
+        in_specs=[vmem] * 6,
+        out_specs=hbm,
+        scratch_shapes=[
+            pltpu.VMEM((tokens, width), BF),
+            dma((BLOCKS,)),
         ],
-        out_specs=pl.BlockSpec((tokens, block), lambda n: (0, n)),
-        scratch_shapes=[
-            pltpu.VMEM((tokens, features), BF),
-            pltpu.VMEM((tokens, 128), F32),
-            pltpu.VMEM((tokens, 128), F32),
-        ],
-        compiler_params=params,
+        compiler_params=params(24),
         name="embed",
-    )(arrived, base, weights, vectors, gram, aux)
+    )(*in_vmem(arrived, base, weights, vectors, gram, aux))
 
 
 def solution(mesh):

time: 55 us -> 49.1 us (0.89)
  local copies, waits for them, and re-layouts: 12.4 us -> 1.56 us
  waiting for transfers between devices: 6.2 us -> 10.4 us
  Pallas kernels: 14.3 us -> 15.2 us
    unnamed x34 -> x4, local copies, waits for them, and re-layouts: 11.6 us -> 1.56 us
    all_to_all x1, waiting for transfers between devices: 6.2 us -> 10.4 us  [body(): lax.all_to_all(message.reshape(shards, 4, 8 * z), ('tile', 'seq'), 0, 0)]
    pallas_call x1, Pallas kernels: 5.49 us -> 6.52 us  [body(): pl.pallas_call(encode_kernel, out_shape=jax.ShapeDtypeStruct((shards * 4,...]
    pallas_call x1, Pallas kernels: 5.18 us -> 4.22 us  [body(): pl.pallas_call(embed_kernel, out_shape=jax.ShapeDtypeStruct((tokens, widt...]
    pallas_call x1, Pallas kernels: 3.6 us -> 4.47 us  [body(): pl.pallas_call(prep_kernel, out_shape=(jax.ShapeDtypeStruct((features, wi...]
    reshape x1 -> x0, local copies, waits for them, and re-layouts: 0.82 us -> none  [body(): row = lambda v: v.reshape(1, -1)]
  transfers between devices with their start and end apart: 1 -> 1, of which waited for: 1 -> 1; matrix products, arithmetic and copies ran while one was open for 0% -> 0% of each run, Pallas kernels for 7% -> 9%
where the time goes in v2:
time: 49.1 us; the launch traced here: 48.9 us
  starting transfers between devices  21.4 us (44%)
  Pallas kernels  15.2 us (31%)
  waiting for transfers between devices  10.4 us (21%)
  local copies, waits for them, and re-layouts  1.56 us (3%)
    all_to_all x1, starting transfers between devices, body(): lax.all_to_all(message.reshape(shards, 4, 8 * z), ('tile', 'seq'), 0, 0)  21.4 us
    all_to_all x1, waiting for transfers between devices, body(): lax.all_to_all(message.reshape(shards, 4, 8 * z), ('tile', 'seq'), 0, 0)  10.4 us
    pallas_call x1, Pallas kernels, body(): pl.pallas_call(encode_kernel, out_shape=jax.ShapeDtypeStruct((shards * 4,...  6.52 us
    pallas_call x1, Pallas kernels, body(): pl.pallas_call(prep_kernel, out_shape=(jax.ShapeDtypeStruct((features, wi...  4.47 us
    pallas_call x1, Pallas kernels, body(): pl.pallas_call(embed_kernel, out_shape=jax.ShapeDtypeStruct((tokens, widt...  4.22 us
    unnamed x4, local copies, waits for them, and re-layouts  1.56 us
  transfers between devices with their start and end apart: 1, of which 1 were waited for; matrix products, arithmetic and copies ran while one was open for 0% of the time, Pallas kernels for 9%

profile of v2, /device:TPU:8, one launch (start us, length us, event | category | flops | bytes accessed | tf_op | source)
XLA Modules:
  0.0 48.9 jit_solution(6427699925707292254)
XLA Ops:
  0.0 6.5 %encode.1 = bf16[1024,128]{1,0:T(8,128)(2,1)} custom-call(s32[1]{0:T(128)} %bitcast.tile_ref, bf16[2,128,8,384]{3,2,1,0:T(8,128)(2,1)} %x_hbm.1, f32[384]{0:T(512)} %gain_hbm.1, bf16[864,384]{1,0:T(8,128)(2,1)} %bitcast.13, f32[16,32]{1,0:T(8,128)} %bitcast.15), custom_call_target="tpu_custom_call" | custom-call | tf_op jit(solution)/shard_map/encode/pallas_call | solution.py:259
  6.5 21.4 %all-to-all-start = ((bf16[256,4,128]{2,1,0:T(4,128)(2,1)}), bf16[256,4,128]{2,1,0:T(4,128)(2,1)S(1)}, u32[]{:S(2)}, u32[]{:S(2)}) async-start(bf16[256,4,128]{2,1,0:T(4,128)(2,1)} %bitcast.3), calls=%async_computation | async-start | bytes 524288 | tf_op jit(solution)/shard_map/all_to_all | solution.py:277
  28.0 4.5 %prep.1 = (bf16[256,5120]{1,0:T(8,128)(2,1)S(1)}, f32[8,5120]{1,0:T(8,128)S(1)}, bf16[256,512]{1,0:T(8,128)(2,1)S(1)}, f32[8,256]{1,0:T(8,128)S(1)}, bf16[512,256]{1,0:T(8,128)(2,1)S(1)}) custom-call(bf16[192,5120]{1,0:T(8,128)(2,1)} %ctx_hbm.1, bf16[64,5120]{1,0:T(8,128)(2,1)} %patch_hbm.1, f32[1,5120]{1,0:T(1,128)} %bitcast.17, f32[1,5120]{1,0:T(1,128)} %bitcast.18, ...), custom_call_target="tpu_custom_call" | custom-call | flops 671088640 | bytes 6000000 | tf_op jit(solution)/shard_map/prep/pallas_call | solution.py:279
  32.5 0.0 copy-start
  32.5 0.6 %copy-done = f32[8,5120]{1,0:T(8,128)} copy-done((f32[8,5120]{1,0:T(8,128)}, f32[8,5120]{1,0:T(8,128)S(1)}, u32[]{:S(2)}) %copy-start) | copy-done | bytes 163864
  33.1 10.4 %all-to-all-done = bf16[256,4,128]{2,1,0:T(4,128)(2,1)S(1)} async-done(((bf16[256,4,128]{2,1,0:T(4,128)(2,1)}), bf16[256,4,128]{2,1,0:T(4,128)(2,1)S(1)}, u32[]{:S(2)}, u32[]{:S(2)}) %all-to-all-start) | async-done | bytes 262176 | tf_op jit(solution)/shard_map/all_to_all | solution.py:277
  43.6 0.0 copy-start.1
  43.6 0.9 %copy-done.1 = f32[8,5120]{1,0:T(8,128)S(1)} copy-done((f32[8,5120]{1,0:T(8,128)S(1)}, f32[8,5120]{1,0:T(8,128)}, u32[]{:S(2)}) %copy-start.1) | copy-done | bytes 163864
  44.5 4.2 %embed.1 = bf16[512,5120]{1,0:T(8,128)(2,1)} custom-call(bf16[1024,128]{1,0:T(8,128)(2,1)S(1)} %bitcast.12, bf16[512,256]{1,0:T(8,128)(2,1)S(1)} %get-tuple-element.10.base_ref, bf16[256,5120]{1,0:T(8,128)(2,1)S(1)} %get-tuple-element.11.w_ref, f32[8,5120]{1,0:T(8,128)S(1)} %copy-done.1, bf16[256,512]{1,0:T(8,128)(2,1)S(1)} %get-tuple-element.13.gram_ref, ...), custom_call_target="tpu_custom_call" | custom-call | tf_op jit(solution)/shard_map/embed/pallas_call | solution.py:308
Async XLA Ops:
  6.5 37.0 %all-to-all-start = ((bf16[256,4,128]{2,1,0:T(4,128)(2,1)}), bf16[256,4,128]{2,1,0:T(4,128)(2,1)S(1)}, u32[]{:S(2)}, u32[]{:S(2)}) async-start(bf16[256,4,128]{2,1,0:T(4,128)(2,1)} %bitcast.3), calls=%async_computation | async-start | bytes 524288 | tf_op jit(solution)/shard_map/all_to_all | solution.py:277
  32.5 0.7 %copy-start = (f32[8,5120]{1,0:T(8,128)}, f32[8,5120]{1,0:T(8,128)S(1)}, u32[]{:S(2)}) copy-start(f32[8,5120]{1,0:T(8,128)S(1)} %get-tuple-element.12.vec_ref) | copy-start | bytes 491524
  43.6 0.9 %copy-start.1 = (f32[8,5120]{1,0:T(8,128)S(1)}, f32[8,5120]{1,0:T(8,128)}, u32[]{:S(2)}) copy-start(f32[8,5120]{1,0:T(8,128)} %copy-done) | copy-start | bytes 491524

commit v3 on v2

--- a/solution.py
+++ b/solution.py
@@ -46,6 +46,7 @@
 
 
 STEP = 8
+CHUNK = 16
 
 
 def encode_kernel(tile_ref, x_hbm, gain_hbm, wt_hbm, mwt_hbm, out_ref, x_ref, gain_ref, wt_ref, mwt_ref, act, big, parts, sem):
@@ -61,17 +62,19 @@
         [(mwt_hbm, mwt_ref), (wt_hbm, wt_ref), (gain_hbm, gain_ref)]
         + [(span(x_hbm, n), span(x_ref, n)) for n in range(blocks)],
     )
-    copies[0].wait()
-    copies[1].wait()
-    pick = (iota((o, taps * o), 1) % o == iota((o, taps * o), 0)).astype(BF)
-    own = iota((taps * z, taps * o), 0) // z == iota((taps * z, taps * o), 1) // o
-    folded = None
-    for part in halves(mwt_ref[...]):
-        spread = dot(part, pick)
-        block = jnp.where(own, jnp.concatenate([spread] * taps, 0), 0.0).astype(BF)
-        term = dot(block, wt_ref[...])
-        folded = term if folded is None else folded + term
-    folded = folded.astype(BF)
+    for copy in copies[: 3 + blocks // 2]:
+        copy.wait()
+    group = 4
+    pick = (iota((o, group * o), 1) % o == iota((o, group * o), 0)).astype(BF)
+    own = iota((group * z, group * o), 0) // z == iota((group * z, group * o), 1) // o
+    spread = [jnp.where(own, jnp.concatenate([dot(part, pick)] * group, 0), 0.0) for part in halves(mwt_ref[...])]
+    spread = jnp.concatenate(spread, 0).astype(BF)
+    folded = []
+    for tap in range(0, taps, group):
+        count = min(group, taps - tap)
+        term = dot(spread[:, : count * o], wt_ref[tap * o : (tap + count) * o])
+        folded.append((term[: count * z] + term[group * z : (group + count) * z]).astype(BF))
+    folded = jnp.concatenate(folded, 0)
     nothing = jnp.zeros((z, channels), BF)
     for t in range(3):
         for slot, (a, e) in enumerate(SLOTS):
@@ -85,28 +88,25 @@
     zero = jnp.zeros((rows, channels), BF)
     act[0, :, :channels] = zero
     act[pairs, :, channels:] = zero
-    step = STEP
-    copies[2].wait()
     gain = gain_ref[...].reshape(1, 1, 1, channels)
-    for j in range(blocks):
-        copies[3 + j].wait()
-        x = x_ref[:, pl.ds(j * 2 * step, 2 * step)].astype(F32)
+    first = tile_ref[0] == 0
+    lanes = 8 * z
+
+    def activate(j):
+        x = x_ref[:, pl.ds(j * 2 * STEP, 2 * STEP)].astype(F32)
         energy = jnp.mean(x * x, axis=-1, keepdims=True)
         v = x * lax.rsqrt(energy + 1e-6) * gain
         v = v * (0.5 + 0.5 * jnp.tanh(0.5 * v))
         v = jnp.concatenate([v[f] for f in range(frames)], axis=1).astype(BF)
-        v = v.reshape(step, 2, rows, channels)
-        act[pl.ds(j * step, step), :, channels:] = v[:, 0]
-        act[pl.ds(j * step + 1, step), :, :channels] = v[:, 1]
-
-    first = tile_ref[0] == 0
-    lanes = 8 * z
-    chunk = 16
-    for c in range(pairs // chunk):
-        low = act[c * chunk : (c + 1) * chunk].reshape(chunk * rows, 2 * channels)
-        high = act[c * chunk + 1 : (c + 1) * chunk + 1].reshape(chunk * rows, 2 * channels)
+        v = v.reshape(STEP, 2, rows, channels)
+        act[pl.ds(j * STEP, STEP), :, channels:] = v[:, 0]
+        act[pl.ds(j * STEP + 1, STEP), :, :channels] = v[:, 1]
+
+    def convolve(c):
+        low = act[c * CHUNK : (c + 1) * CHUNK].reshape(CHUNK * rows, 2 * channels)
+        high = act[c * CHUNK + 1 : (c + 1) * CHUNK + 1].reshape(CHUNK * rows, 2 * channels)
         out = dot_nt(low, big[:, : 2 * channels]) + dot_nt(high, big[:, 2 * channels :])
-        out = out.reshape(chunk // 2, 2, frames, columns, 3 * lanes)
+        out = out.reshape(CHUNK // 2, 2, frames, columns, 3 * lanes)
         part = lambda p, f, t: out[:, p, f, :, t * lanes : (t + 1) * lanes]
         for p in range(2):
             ext = (
@@ -122,9 +122,22 @@
                 jnp.where(first, ext[3], ext[1]),
             )
             for f in range(4):
-                at = ((p * 4 + f) * (pairs // 2) + c * chunk // 2) * columns
-                size = chunk // 2 * columns
+                at = ((p * 4 + f) * (pairs // 2) + c * CHUNK // 2) * columns
+                size = CHUNK // 2 * columns
                 parts[at : at + size] = slots[f].reshape(size, lanes)
+
+    done = 0
+    for j in range(blocks):
+        if j == blocks // 2:
+            for copy in copies[3 + blocks // 2 :]:
+                copy.wait()
+        activate(j)
+        while (done + 1) * CHUNK + 1 <= (j + 1) * STEP:
+            convolve(done)
+            done += 1
+    while done * CHUNK < pairs:
+        convolve(done)
+        done += 1
 
     total = parts.shape[0]
     even = parts[pl.ds(0, total // 2, stride=2)]
@@ -139,13 +152,13 @@
 
 def prep_kernel(
     ctx_hbm, patch_hbm, pb_hbm, cb_hbm, shift_hbm, scale_hbm, noisy_hbm, mask_hbm, conv_bias_hbm, mwt_hbm, mb_hbm,
-    w_ref, vec_ref, gram_ref, aux_ref, base_ref,
+    w_ref, gram_ref, aux_ref, base_ref,
     ctx_ref, rows_ref, noisy_ref, conv_bias_ref, mwt_ref, mb_ref, sem,
 ):
     z = mwt_ref.shape[0]
     lat = 4 * z
     width = w_ref.shape[1]
-    size = w_ref.shape[0]
+    size = 4 * lat
     copies = fetch(
         sem,
         [
@@ -171,11 +184,10 @@
     bias = rows_ref[0] + rows_ref[1]
     mean_b = jnp.mean(bias, axis=1, keepdims=True)
     centred = bias - mean_b
-    vec_ref[0:1] = bias
-    vec_ref[1:2] = 1.0 + rows_ref[3]
-    vec_ref[2:3] = rows_ref[2]
-    vec_ref[3:8] = jnp.zeros((5, width), F32)
-    w = w_ref[...]
+    gain = 1.0 + rows_ref[3]
+    vectors = (*halves(centred * gain), *halves(rows_ref[2]))
+    w_ref[size:] = jnp.concatenate([*vectors, jnp.zeros((VECTORS - 4, width), BF)], 0)
+    w = w_ref[:size]
     high, low = halves(centred)
     rows = jnp.concatenate([jnp.ones((1, width), BF), high, low, jnp.zeros((5, width), BF)], 0)
     sums = dot_nt(rows, w)
@@ -191,21 +203,21 @@
     conv_bias = jnp.broadcast_to(conv_bias_ref[...], (8, conv_bias_ref.shape[1]))
     latent_bias = lax.dot_general(conv_bias, tiled, NT, precision=lax.Precision.HIGHEST, preferred_element_type=F32)
     latent_bias = latent_bias[:1] + jnp.concatenate([mb_ref[...]] * 8, 1)
-    aux_ref[0:1] = mean_w
-    aux_ref[1:2] = 2.0 * (sums[1:2] + sums[2:3]) / width
-    aux_ref[2:3] = jnp.broadcast_to(mean_b, (1, size))
-    aux_ref[3:4] = jnp.broadcast_to(square, (1, size))
-    aux_ref[4:5] = jnp.concatenate([latent_bias] * (size // latent_bias.shape[1]), 1)
-    aux_ref[5:8] = jnp.zeros((3, size), F32)
+    aux_ref[0:1] = 2.0 * (sums[1:2] + sums[2:3]) / width
+    aux_ref[1:2] = jnp.broadcast_to(square, (1, size))
+    aux_ref[2:3] = jnp.concatenate([latent_bias] * (size // latent_bias.shape[1]), 1)
+    aux_ref[3:8] = jnp.zeros((5, size), F32)
+    w_ref[:size] = ((w.astype(F32) - mean_col) * gain).astype(BF)
     place = (iota((lat, 2 * lat), 1) == iota((lat, 2 * lat), 0) + lat).astype(BF)
     noisy = lax.dot_general(noisy_ref[...], place, (((0,), (0,)), ((), ())), preferred_element_type=F32)
     base_ref[:, : 2 * lat] = noisy.astype(BF)
 
 
+VECTORS = 16
 BLOCKS = 10
 
 
-def embed_kernel(arrived_ref, base_ref, w_ref, vec_ref, gram_ref, aux_ref, out_hbm, out_ref, sem):
+def embed_kernel(arrived_ref, base_ref, w_ref, gram_ref, aux_ref, out_hbm, out_ref, sem):
     block = w_ref.shape[1] // BLOCKS
     columns = lambda n: pl.ds(n * block, block)
     tokens = base_ref.shape[0]
@@ -217,21 +229,23 @@
     down = jnp.where(row == 0, 0.0, pltpu.roll(crossed, 1, 0))
     up = jnp.where(row == tokens - 1, 0.0, pltpu.roll(crossed, tokens - 1, 0))
     lane = iota((1, lanes), 1)
-    latent = both + jnp.where(lane // z % 2 == 0, down, up) + aux_ref[4:5, :lanes]
+    latent = both + jnp.where(lane // z % 2 == 0, down, up) + aux_ref[2:3, :lanes]
     front = jnp.where(lane < lanes // 2, latent, base_ref[:, :lanes].astype(F32))
     x = jnp.concatenate([front.astype(BF), base_ref[:, lanes:]], 1)
     size = x.shape[1]
-    y = dot(x, gram_ref[:, :size]) + dot(x, gram_ref[:, size:])
-    xf = x.astype(F32)
-    mean = jnp.sum(xf * aux_ref[0:1], axis=1, keepdims=True) + aux_ref[2:3, :1]
-    variance = jnp.sum((y + aux_ref[1:2]) * xf, axis=1, keepdims=True) + aux_ref[3:4, :1]
-    scale = lax.rsqrt(jnp.maximum(variance, 0.0) + 1e-6)
-    offset = mean * scale
+    scales = []
+    for r in range(0, tokens, 256):
+        xr = x[r : r + 256]
+        y = dot(xr, gram_ref[:, :size]) + dot(xr, gram_ref[:, size:])
+        variance = jnp.sum((y + aux_ref[0:1]) * xr.astype(F32), axis=1, keepdims=True) + aux_ref[1:2, :1]
+        scales.append(lax.rsqrt(jnp.maximum(variance, 0.0) + 1e-6))
+    scale = jnp.concatenate(scales, 0)
     sent = []
     for n in range(BLOCKS):
         at = slice(n * block, (n + 1) * block)
-        combined = dot(x, w_ref[:, at]) + vec_ref[0:1, at]
-        out_ref[:, at] = ((combined * scale - offset) * vec_ref[1:2, at] + vec_ref[2:3, at]).astype(BF)
+        vectors = w_ref[size:, at].astype(F32)
+        centred = dot(x, w_ref[:size, at]) + (vectors[0:1] + vectors[1:2])
+        out_ref[:, at] = (centred * scale + (vectors[2:3] + vectors[3:4])).astype(BF)
         copy = pltpu.make_async_copy(out_ref.at[:, columns(n)], out_hbm.at[:, columns(n)], sem.at[n])
         copy.start()
         sent.append(copy)
@@ -276,17 +290,16 @@
     )(tile, *in_hbm(section_input, norm_gain, conv_weight.T, mean_weight.T))
     arrived = lax.all_to_all(message.reshape(shards, 4, 8 * z), ("tile", "seq"), 0, 0)
     arrived = arrived.reshape(shards * 4, 8 * z)
-    weights, vectors, gram, aux, base = pl.pallas_call(
+    weights, gram, aux, base = pl.pallas_call(
         prep_kernel,
         out_shape=(
-            jax.ShapeDtypeStruct((features, width), BF),
-            jax.ShapeDtypeStruct((8, width), F32),
+            jax.ShapeDtypeStruct((features + VECTORS, width), BF),
             jax.ShapeDtypeStruct((features, 2 * features), BF),
             jax.ShapeDtypeStruct((8, features), F32),
             jax.ShapeDtypeStruct((tokens, features), BF),
         ),
         in_specs=[hbm] * 11,
-        out_specs=(vmem,) * 5,
+        out_specs=(vmem,) * 4,
         scratch_shapes=[
             pltpu.VMEM((4 * z, width), BF),
             pltpu.VMEM((4, 1, width), F32),
@@ -308,7 +321,7 @@
     return pl.pallas_call(
         embed_kernel,
         out_shape=jax.ShapeDtypeStruct((tokens, width), BF),
-        in_specs=[vmem] * 6,
+        in_specs=[vmem] * 5,
         out_specs=hbm,
         scratch_shapes=[
             pltpu.VMEM((tokens, width), BF),
@@ -316,7 +329,7 @@
         ],
         compiler_params=params(24),
         name="embed",
-    )(*in_vmem(arrived, base, weights, vectors, gram, aux))
+    )(*in_vmem(arrived, base, weights, gram, aux))
 
 
 def solution(mesh):

time: 49.1 us -> 46.4 us (0.945)
  Pallas kernels: 15.2 us -> 13.3 us
  waiting for transfers between devices: 10.4 us -> 9.78 us
    pallas_call x1, Pallas kernels: 6.52 us -> 5.09 us  [body(): pl.pallas_call(encode_kernel, out_shape=jax.ShapeDtypeStruct((shards * 4,...]
    pallas_call x1, Pallas kernels: 4.22 us -> 3.1 us  [body(): pl.pallas_call(embed_kernel, out_shape=jax.ShapeDtypeStruct((tokens, widt...]
    all_to_all x1, waiting for transfers between devices: 10.4 us -> 9.78 us  [body(): lax.all_to_all(message.reshape(shards, 4, 8 * z), ('tile', 'seq'), 0, 0)]
    pallas_call x1, Pallas kernels: 4.47 us -> 5.09 us  [body(): pl.pallas_call(prep_kernel, out_shape=(jax.ShapeDtypeStruct((features + V...]
  transfers between devices with their start and end apart: 1 -> 1, of which waited for: 1 -> 1; matrix products, arithmetic and copies ran while one was open for 0% -> 0% of each run, Pallas kernels for 9% -> 11%
where the time goes in v3:
time: 46.4 us; the launch traced here: 46.2 us
  starting transfers between devices  21.4 us (46%)
  Pallas kernels  13.3 us (29%)
  waiting for transfers between devices  9.78 us (21%)
  local copies, waits for them, and re-layouts  1.63 us (4%)
    all_to_all x1, starting transfers between devices, body(): lax.all_to_all(message.reshape(shards, 4, 8 * z), ('tile', 'seq'), 0, 0)  21.4 us
    all_to_all x1, waiting for transfers between devices, body(): lax.all_to_all(message.reshape(shards, 4, 8 * z), ('tile', 'seq'), 0, 0)  9.78 us
    pallas_call x1, Pallas kernels, body(): pl.pallas_call(encode_kernel, out_shape=jax.ShapeDtypeStruct((shards * 4,...  5.09 us
    pallas_call x1, Pallas kernels, body(): pl.pallas_call(prep_kernel, out_shape=(jax.ShapeDtypeStruct((features + V...  5.09 us
    pallas_call x1, Pallas kernels, body(): pl.pallas_call(embed_kernel, out_shape=jax.ShapeDtypeStruct((tokens, widt...  3.1 us
    unnamed x4, local copies, waits for them, and re-layouts  1.63 us
  transfers between devices with their start and end apart: 1, of which 1 were waited for; matrix products, arithmetic and copies ran while one was open for 0% of the time, Pallas kernels for 11%

profile of v3, /device:TPU:8, one launch (start us, length us, event | category | flops | bytes accessed | tf_op | source)
XLA Modules:
  0.0 46.2 jit_solution(14851856396638393318)
XLA Ops:
  0.0 5.1 %encode.1 = bf16[1024,128]{1,0:T(8,128)(2,1)} custom-call(s32[1]{0:T(128)} %bitcast.tile_ref, bf16[2,128,8,384]{3,2,1,0:T(8,128)(2,1)} %x_hbm.1, f32[384]{0:T(512)} %gain_hbm.1, bf16[864,384]{1,0:T(8,128)(2,1)} %bitcast.13, f32[16,32]{1,0:T(8,128)} %bitcast.15), custom_call_target="tpu_custom_call" | custom-call | tf_op jit(solution)/shard_map/encode/pallas_call | solution.py:273
  5.1 21.4 %all-to-all-start = ((bf16[256,4,128]{2,1,0:T(4,128)(2,1)}), bf16[256,4,128]{2,1,0:T(4,128)(2,1)S(1)}, u32[]{:S(2)}, u32[]{:S(2)}) async-start(bf16[256,4,128]{2,1,0:T(4,128)(2,1)} %bitcast.3), calls=%async_computation | async-start | bytes 524288 | tf_op jit(solution)/shard_map/all_to_all | solution.py:291
  26.6 5.1 %prep.1 = (bf16[272,5120]{1,0:T(8,128)(2,1)S(1)}, bf16[256,512]{1,0:T(8,128)(2,1)S(1)}, f32[8,256]{1,0:T(8,128)S(1)}, bf16[512,256]{1,0:T(8,128)(2,1)S(1)}) custom-call(bf16[192,5120]{1,0:T(8,128)(2,1)} %ctx_hbm.1, bf16[64,5120]{1,0:T(8,128)(2,1)} %patch_hbm.1, f32[1,5120]{1,0:T(1,128)} %bitcast.17, f32[1,5120]{1,0:T(1,128)} %bitcast.18, ...), custom_call_target="tpu_custom_call" | custom-call | flops 671088640 | bytes 6000000 | tf_op jit(solution)/shard_map/prep/pallas_call | solution.py:293
  31.6 0.0 copy-start
  31.7 0.7 %copy-done = bf16[512,256]{1,0:T(8,128)(2,1)} copy-done((bf16[512,256]{1,0:T(8,128)(2,1)}, bf16[512,256]{1,0:T(8,128)(2,1)S(1)}, u32[]{:S(2)}) %copy-start) | copy-done | bytes 262168
  32.3 9.8 %all-to-all-done = bf16[256,4,128]{2,1,0:T(4,128)(2,1)S(1)} async-done(((bf16[256,4,128]{2,1,0:T(4,128)(2,1)}), bf16[256,4,128]{2,1,0:T(4,128)(2,1)S(1)}, u32[]{:S(2)}, u32[]{:S(2)}) %all-to-all-start) | async-done | bytes 262176 | tf_op jit(solution)/shard_map/all_to_all | solution.py:291
  42.1 0.0 copy-start.1
  42.1 0.9 %copy-done.1 = bf16[512,256]{1,0:T(8,128)(2,1)S(1)} copy-done((bf16[512,256]{1,0:T(8,128)(2,1)S(1)}, bf16[512,256]{1,0:T(8,128)(2,1)}, u32[]{:S(2)}) %copy-start.1) | copy-done | bytes 262168
  43.1 3.1 %embed.1 = bf16[512,5120]{1,0:T(8,128)(2,1)} custom-call(bf16[1024,128]{1,0:T(8,128)(2,1)S(1)} %bitcast.12, bf16[512,256]{1,0:T(8,128)(2,1)S(1)} %copy-done.1, bf16[272,5120]{1,0:T(8,128)(2,1)S(1)} %get-tuple-element.10.w_ref, bf16[256,512]{1,0:T(8,128)(2,1)S(1)} %get-tuple-element.11.gram_ref, f32[8,256]{1,0:T(8,128)S(1)} %get-tuple-element.12.aux_ref), custom_call_target="tpu_custom_call" | custom-call | tf_op jit(solution)/shard_map/embed/pallas_call | solution.py:321
Async XLA Ops:
  5.1 37.0 %all-to-all-start = ((bf16[256,4,128]{2,1,0:T(4,128)(2,1)}), bf16[256,4,128]{2,1,0:T(4,128)(2,1)S(1)}, u32[]{:S(2)}, u32[]{:S(2)}) async-start(bf16[256,4,128]{2,1,0:T(4,128)(2,1)} %bitcast.3), calls=%async_computation | async-start | bytes 524288 | tf_op jit(solution)/shard_map/all_to_all | solution.py:291
  31.6 0.7 %copy-start = (bf16[512,256]{1,0:T(8,128)(2,1)}, bf16[512,256]{1,0:T(8,128)(2,1)S(1)}, u32[]{:S(2)}) copy-start(bf16[512,256]{1,0:T(8,128)(2,1)S(1)} %get-tuple-element.9.base_ref) | copy-start | bytes 786436
  42.1 1.0 %copy-start.1 = (bf16[512,256]{1,0:T(8,128)(2,1)S(1)}, bf16[512,256]{1,0:T(8,128)(2,1)}, u32[]{:S(2)}) copy-start(bf16[512,256]{1,0:T(8,128)(2,1)} %copy-done) | copy-start | bytes 786436

commit v4 on v3

--- a/solution.py
+++ b/solution.py
@@ -46,10 +46,10 @@
 
 
 STEP = 8
-CHUNK = 16
-
-
-def encode_kernel(tile_ref, x_hbm, gain_hbm, wt_hbm, mwt_hbm, out_ref, x_ref, gain_ref, wt_ref, mwt_ref, act, big, parts, sem):
+CHUNK = 32
+
+
+def encode_kernel(tile_ref, x_hbm, gain_hbm, wt_hbm, mwt_hbm, out_ref, x_ref, gain_ref, wt_ref, mwt_ref, act, big, side, parts, sem):
     frames, height, columns, channels = x_ref.shape
     pairs = height // 2
     rows = frames * columns
@@ -76,6 +76,7 @@
         folded.append((term[: count * z] + term[group * z : (group + count) * z]).astype(BF))
     folded = jnp.concatenate(folded, 0)
     nothing = jnp.zeros((z, channels), BF)
+    lanes = 8 * z
     for t in range(3):
         for slot, (a, e) in enumerate(SLOTS):
             at = (t * 8 + slot) * z
@@ -83,15 +84,17 @@
                 b = k - a
                 tap = ((t * 3 + b) * 3 + e) * z
                 value = folded[tap : tap + z] if 0 <= b < 3 else nothing
-                big[at : at + z, k * channels : (k + 1) * channels] = value
+                if t:
+                    big[at - lanes : at - lanes + z, k * channels : (k + 1) * channels] = value
+                else:
+                    row = at + k // 2 * lanes
+                    side[row : row + z, k % 2 * channels : (k % 2 + 1) * channels] = value
 
     zero = jnp.zeros((rows, channels), BF)
     act[0, :, :channels] = zero
     act[pairs, :, channels:] = zero
     gain = gain_ref[...].reshape(1, 1, 1, channels)
     first = tile_ref[0] == 0
-    lanes = 8 * z
-
     def activate(j):
         x = x_ref[:, pl.ds(j * 2 * STEP, 2 * STEP)].astype(F32)
         energy = jnp.mean(x * x, axis=-1, keepdims=True)
@@ -103,11 +106,13 @@
         act[pl.ds(j * STEP + 1, STEP), :, :channels] = v[:, 1]
 
     def convolve(c):
-        low = act[c * CHUNK : (c + 1) * CHUNK].reshape(CHUNK * rows, 2 * channels)
-        high = act[c * CHUNK + 1 : (c + 1) * CHUNK + 1].reshape(CHUNK * rows, 2 * channels)
-        out = dot_nt(low, big[:, : 2 * channels]) + dot_nt(high, big[:, 2 * channels :])
-        out = out.reshape(CHUNK // 2, 2, frames, columns, 3 * lanes)
-        part = lambda p, f, t: out[:, p, f, :, t * lanes : (t + 1) * lanes]
+        both = act[c * CHUNK : (c + 1) * CHUNK + 1].reshape((CHUNK + 1) * rows, 2 * channels)
+        low, high = both[:-rows], both[rows:]
+        later = dot_nt(low, big[:, : 2 * channels]) + dot_nt(high, big[:, 2 * channels :])
+        now = dot_nt(both, side[...])
+        outs = (now[:-rows, :lanes] + now[rows:, lanes:], later[:, :lanes], later[:, lanes:])
+        outs = [out.reshape(CHUNK // 2, 2, frames, columns, lanes) for out in outs]
+        part = lambda p, f, t: outs[t][:, p, f]
         for p in range(2):
             ext = (
                 part(p, 0, 2),
@@ -152,13 +157,13 @@
 
 def prep_kernel(
     ctx_hbm, patch_hbm, pb_hbm, cb_hbm, shift_hbm, scale_hbm, noisy_hbm, mask_hbm, conv_bias_hbm, mwt_hbm, mb_hbm,
-    w_ref, gram_ref, aux_ref, base_ref,
+    w_ref, vec_ref, gram_ref, aux_ref, base_ref,
     ctx_ref, rows_ref, noisy_ref, conv_bias_ref, mwt_ref, mb_ref, sem,
 ):
     z = mwt_ref.shape[0]
     lat = 4 * z
     width = w_ref.shape[1]
-    size = 4 * lat
+    size = w_ref.shape[0]
     copies = fetch(
         sem,
         [
@@ -185,9 +190,9 @@
     mean_b = jnp.mean(bias, axis=1, keepdims=True)
     centred = bias - mean_b
     gain = 1.0 + rows_ref[3]
-    vectors = (*halves(centred * gain), *halves(rows_ref[2]))
-    w_ref[size:] = jnp.concatenate([*vectors, jnp.zeros((VECTORS - 4, width), BF)], 0)
-    w = w_ref[:size]
+    vec_ref[0:1] = centred * gain
+    vec_ref[1:2] = rows_ref[2]
+    w = w_ref[...]
     high, low = halves(centred)
     rows = jnp.concatenate([jnp.ones((1, width), BF), high, low, jnp.zeros((5, width), BF)], 0)
     sums = dot_nt(rows, w)
@@ -207,17 +212,16 @@
     aux_ref[1:2] = jnp.broadcast_to(square, (1, size))
     aux_ref[2:3] = jnp.concatenate([latent_bias] * (size // latent_bias.shape[1]), 1)
     aux_ref[3:8] = jnp.zeros((5, size), F32)
-    w_ref[:size] = ((w.astype(F32) - mean_col) * gain).astype(BF)
+    w_ref[...] = ((w.astype(F32) - mean_col) * gain).astype(BF)
     place = (iota((lat, 2 * lat), 1) == iota((lat, 2 * lat), 0) + lat).astype(BF)
     noisy = lax.dot_general(noisy_ref[...], place, (((0,), (0,)), ((), ())), preferred_element_type=F32)
     base_ref[:, : 2 * lat] = noisy.astype(BF)
 
 
-VECTORS = 16
 BLOCKS = 10
 
 
-def embed_kernel(arrived_ref, base_ref, w_ref, gram_ref, aux_ref, out_hbm, out_ref, sem):
+def embed_kernel(arrived_ref, base_ref, w_ref, vec_ref, gram_ref, aux_ref, out_hbm, out_ref, sem):
     block = w_ref.shape[1] // BLOCKS
     columns = lambda n: pl.ds(n * block, block)
     tokens = base_ref.shape[0]
@@ -243,9 +247,8 @@
     sent = []
     for n in range(BLOCKS):
         at = slice(n * block, (n + 1) * block)
-        vectors = w_ref[size:, at].astype(F32)
-        centred = dot(x, w_ref[:size, at]) + (vectors[0:1] + vectors[1:2])
-        out_ref[:, at] = (centred * scale + (vectors[2:3] + vectors[3:4])).astype(BF)
+        centred = dot(x, w_ref[:, at]) + vec_ref[0:1, at]
+        out_ref[:, at] = (centred * scale + vec_ref[1:2, at]).astype(BF)
         copy = pltpu.make_async_copy(out_ref.at[:, columns(n)], out_hbm.at[:, columns(n)], sem.at[n])
         copy.start()
         sent.append(copy)
@@ -281,7 +284,8 @@
             pltpu.VMEM((taps_out, channels), BF),
             pltpu.VMEM(mean_weight.shape[::-1], F32),
             pltpu.VMEM((height // 2 + 1, frames * columns, 2 * channels), BF),
-            pltpu.VMEM((3 * 8 * z, 4 * channels), BF),
+            pltpu.VMEM((2 * 8 * z, 4 * channels), BF),
+            pltpu.VMEM((2 * 8 * z, 2 * channels), BF),
             pltpu.VMEM((shards * 8, 8 * z), F32),
             dma((3 + height // 2 // STEP,)),
         ],
@@ -290,16 +294,17 @@
     )(tile, *in_hbm(section_input, norm_gain, conv_weight.T, mean_weight.T))
     arrived = lax.all_to_all(message.reshape(shards, 4, 8 * z), ("tile", "seq"), 0, 0)
     arrived = arrived.reshape(shards * 4, 8 * z)
-    weights, gram, aux, base = pl.pallas_call(
+    weights, vectors, gram, aux, base = pl.pallas_call(
         prep_kernel,
         out_shape=(
-            jax.ShapeDtypeStruct((features + VECTORS, width), BF),
+            jax.ShapeDtypeStruct((features, width), BF),
+            jax.ShapeDtypeStruct((2, width), F32),
             jax.ShapeDtypeStruct((features, 2 * features), BF),
             jax.ShapeDtypeStruct((8, features), F32),
             jax.ShapeDtypeStruct((tokens, features), BF),
         ),
         in_specs=[hbm] * 11,
-        out_specs=(vmem,) * 4,
+        out_specs=(vmem,) * 5,
         scratch_shapes=[
             pltpu.VMEM((4 * z, width), BF),
             pltpu.VMEM((4, 1, width), F32),
@@ -321,7 +326,7 @@
     return pl.pallas_call(
         embed_kernel,
         out_shape=jax.ShapeDtypeStruct((tokens, width), BF),
-        in_specs=[vmem] * 5,
+        in_specs=[vmem] * 6,
         out_specs=hbm,
         scratch_shapes=[
             pltpu.VMEM((tokens, width), BF),
@@ -329,7 +334,7 @@
         ],
         compiler_params=params(24),
         name="embed",
-    )(*in_vmem(arrived, base, weights, gram, aux))
+    )(*in_vmem(arrived, base, weights, vectors, gram, aux))
 
 
 def solution(mesh):

time: 46.4 us -> 45 us (0.970)
  local copies, waits for them, and re-layouts: 1.63 us -> 0 us
  waiting for transfers between devices: 9.78 us -> 10.5 us
  Pallas kernels: 13.3 us -> 12.8 us
    unnamed x4 -> x0, local copies, waits for them, and re-layouts: 1.63 us -> none
    all_to_all x1, waiting for transfers between devices: 9.78 us -> 10.5 us  [body(): lax.all_to_all(message.reshape(shards, 4, 8 * z), ('tile', 'seq'), 0, 0)]
where the time goes in v4:
time: 45 us; the launch traced here: 44.8 us
  starting transfers between devices  21.4 us (48%)
  Pallas kernels  12.8 us (28%)
  waiting for transfers between devices  10.5 us (23%)
    all_to_all x1, starting transfers between devices, body(): lax.all_to_all(message.reshape(shards, 4, 8 * z), ('tile', 'seq'), 0, 0)  21.4 us
    all_to_all x1, waiting for transfers between devices, body(): lax.all_to_all(message.reshape(shards, 4, 8 * z), ('tile', 'seq'), 0, 0)  10.5 us
    pallas_call x1, Pallas kernels, body(): pl.pallas_call(prep_kernel, out_shape=(jax.ShapeDtypeStruct((features, wi...  5.02 us
    pallas_call x1, Pallas kernels, body(): pl.pallas_call(encode_kernel, out_shape=jax.ShapeDtypeStruct((shards * 4,...  4.67 us
    pallas_call x1, Pallas kernels, body(): pl.pallas_call(embed_kernel, out_shape=jax.ShapeDtypeStruct((tokens, widt...  3.1 us
  transfers between devices with their start and end apart: 1, of which 1 were waited for; matrix products, arithmetic and copies ran while one was open for 0% of the time, Pallas kernels for 11%

profile of v4, /device:TPU:8, one launch (start us, length us, event | category | flops | bytes accessed | tf_op | source)
XLA Modules:
  0.0 44.8 jit_solution(14916122103101181182)
XLA Ops:
  0.0 4.7 %encode.1 = bf16[1024,128]{1,0:T(8,128)(2,1)} custom-call(s32[1]{0:T(128)} %bitcast.tile_ref, bf16[2,128,8,384]{3,2,1,0:T(8,128)(2,1)} %x_hbm.1, f32[384]{0:T(512)} %gain_hbm.1, bf16[864,384]{1,0:T(8,128)(2,1)} %bitcast.13, f32[16,32]{1,0:T(8,128)} %bitcast.15), custom_call_target="tpu_custom_call" | custom-call | tf_op jit(solution)/shard_map/encode/pallas_call | solution.py:276
  4.7 21.4 %all-to-all-start = ((bf16[256,4,128]{2,1,0:T(4,128)(2,1)}), bf16[256,4,128]{2,1,0:T(4,128)(2,1)S(1)}, u32[]{:S(2)}, u32[]{:S(2)}) async-start(bf16[256,4,128]{2,1,0:T(4,128)(2,1)} %bitcast.3), calls=%async_computation | async-start | bytes 524288 | tf_op jit(solution)/shard_map/all_to_all | solution.py:295
  26.1 5.0 %prep.1 = (bf16[256,5120]{1,0:T(8,128)(2,1)S(1)}, f32[2,5120]{1,0:T(2,128)S(1)}, bf16[256,512]{1,0:T(8,128)(2,1)S(1)}, f32[8,256]{1,0:T(8,128)S(1)}, bf16[512,256]{1,0:T(8,128)(2,1)S(1)}) custom-call(bf16[192,5120]{1,0:T(8,128)(2,1)} %ctx_hbm.1, bf16[64,5120]{1,0:T(8,128)(2,1)} %patch_hbm.1, f32[1,5120]{1,0:T(1,128)} %bitcast.17, f32[1,5120]{1,0:T(1,128)} %bitcast.18, ...), custom_call_target="tpu_custom_call" | custom-call | flops 671088640 | bytes 6000000 | tf_op jit(solution)/shard_map/prep/pallas_call | solution.py:297
  31.2 10.5 %all-to-all-done = bf16[256,4,128]{2,1,0:T(4,128)(2,1)S(1)} async-done(((bf16[256,4,128]{2,1,0:T(4,128)(2,1)}), bf16[256,4,128]{2,1,0:T(4,128)(2,1)S(1)}, u32[]{:S(2)}, u32[]{:S(2)}) %all-to-all-start) | async-done | bytes 262176 | tf_op jit(solution)/shard_map/all_to_all | solution.py:295
  41.7 3.1 %embed.1 = bf16[512,5120]{1,0:T(8,128)(2,1)} custom-call(bf16[1024,128]{1,0:T(8,128)(2,1)S(1)} %bitcast.12, bf16[512,256]{1,0:T(8,128)(2,1)S(1)} %get-tuple-element.10.base_ref, bf16[256,5120]{1,0:T(8,128)(2,1)S(1)} %get-tuple-element.11.w_ref, f32[2,5120]{1,0:T(2,128)S(1)} %get-tuple-element.12.vec_ref, bf16[256,512]{1,0:T(8,128)(2,1)S(1)} %get-tuple-element.13.gram_ref, ...), custom_call_target="tpu_custom_call" | custom-call | tf_op jit(solution)/shard_map/embed/pallas_call | solution.py:326
Async XLA Ops:
  4.7 37.0 %all-to-all-start = ((bf16[256,4,128]{2,1,0:T(4,128)(2,1)}), bf16[256,4,128]{2,1,0:T(4,128)(2,1)S(1)}, u32[]{:S(2)}, u32[]{:S(2)}) async-start(bf16[256,4,128]{2,1,0:T(4,128)(2,1)} %bitcast.3), calls=%async_computation | async-start | bytes 524288 | tf_op jit(solution)/shard_map/all_to_all | solution.py:295

commit v5 on v4

--- a/solution.py
+++ b/solution.py
@@ -62,7 +62,7 @@
         [(mwt_hbm, mwt_ref), (wt_hbm, wt_ref), (gain_hbm, gain_ref)]
         + [(span(x_hbm, n), span(x_ref, n)) for n in range(blocks)],
     )
-    for copy in copies[: 3 + blocks // 2]:
+    for copy in copies[: 3 + 2]:
         copy.wait()
     group = 4
     pick = (iota((o, group * o), 1) % o == iota((o, group * o), 0)).astype(BF)
@@ -93,13 +93,13 @@
     zero = jnp.zeros((rows, channels), BF)
     act[0, :, :channels] = zero
     act[pairs, :, channels:] = zero
-    gain = gain_ref[...].reshape(1, 1, 1, channels)
+    gain = 0.5 * gain_ref[...].reshape(1, 1, 1, channels)
     first = tile_ref[0] == 0
     def activate(j):
         x = x_ref[:, pl.ds(j * 2 * STEP, 2 * STEP)].astype(F32)
         energy = jnp.mean(x * x, axis=-1, keepdims=True)
-        v = x * lax.rsqrt(energy + 1e-6) * gain
-        v = v * (0.5 + 0.5 * jnp.tanh(0.5 * v))
+        u = x * lax.rsqrt(energy + 1e-6) * gain
+        v = u + u * jnp.tanh(u)
         v = jnp.concatenate([v[f] for f in range(frames)], axis=1).astype(BF)
         v = v.reshape(STEP, 2, rows, channels)
         act[pl.ds(j * STEP, STEP), :, channels:] = v[:, 0]
@@ -133,8 +133,8 @@
 
     done = 0
     for j in range(blocks):
-        if j == blocks // 2:
-            for copy in copies[3 + blocks // 2 :]:
+        if j == 2:
+            for copy in copies[3 + 2 :]:
                 copy.wait()
         activate(j)
         while (done + 1) * CHUNK + 1 <= (j + 1) * STEP:

time: 45 us -> 44.6 us (level)
  Pallas kernels: 12.8 us -> 12.3 us
    pallas_call x1, Pallas kernels: 4.67 us -> 4.22 us  [body(): pl.pallas_call(encode_kernel, out_shape=jax.ShapeDtypeStruct((shards * 4,...]
where the time goes in v5:
time: 44.6 us; the launch traced here: 44.3 us
  starting transfers between devices  21.4 us (48%)
  Pallas kernels  12.3 us (28%)
  waiting for transfers between devices  10.5 us (24%)
    all_to_all x1, starting transfers between devices, body(): lax.all_to_all(message.reshape(shards, 4, 8 * z), ('tile', 'seq'), 0, 0)  21.4 us
    all_to_all x1, waiting for transfers between devices, body(): lax.all_to_all(message.reshape(shards, 4, 8 * z), ('tile', 'seq'), 0, 0)  10.5 us
    pallas_call x1, Pallas kernels, body(): pl.pallas_call(prep_kernel, out_shape=(jax.ShapeDtypeStruct((features, wi...  5.02 us
    pallas_call x1, Pallas kernels, body(): pl.pallas_call(encode_kernel, out_shape=jax.ShapeDtypeStruct((shards * 4,...  4.22 us
    pallas_call x1, Pallas kernels, body(): pl.pallas_call(embed_kernel, out_shape=jax.ShapeDtypeStruct((tokens, widt...  3.1 us
  transfers between devices with their start and end apart: 1, of which 1 were waited for; matrix products, arithmetic and copies ran while one was open for 0% of the time, Pallas kernels for 11%

profile of v5, /device:TPU:8, one launch (start us, length us, event | category | flops | bytes accessed | tf_op | source)
XLA Modules:
  0.0 44.3 jit_solution(9421021756660921326)
XLA Ops:
  0.0 4.2 %encode.1 = bf16[1024,128]{1,0:T(8,128)(2,1)} custom-call(s32[1]{0:T(128)} %bitcast.tile_ref, bf16[2,128,8,384]{3,2,1,0:T(8,128)(2,1)} %x_hbm.1, f32[384]{0:T(512)} %gain_hbm.1, bf16[864,384]{1,0:T(8,128)(2,1)} %bitcast.13, f32[16,32]{1,0:T(8,128)} %bitcast.15), custom_call_target="tpu_custom_call" | custom-call | tf_op jit(solution)/shard_map/encode/pallas_call | solution.py:276
  4.2 21.4 %all-to-all-start = ((bf16[256,4,128]{2,1,0:T(4,128)(2,1)}), bf16[256,4,128]{2,1,0:T(4,128)(2,1)S(1)}, u32[]{:S(2)}, u32[]{:S(2)}) async-start(bf16[256,4,128]{2,1,0:T(4,128)(2,1)} %bitcast.3), calls=%async_computation | async-start | bytes 524288 | tf_op jit(solution)/shard_map/all_to_all | solution.py:295
  25.7 5.0 %prep.1 = (bf16[256,5120]{1,0:T(8,128)(2,1)S(1)}, f32[2,5120]{1,0:T(2,128)S(1)}, bf16[256,512]{1,0:T(8,128)(2,1)S(1)}, f32[8,256]{1,0:T(8,128)S(1)}, bf16[512,256]{1,0:T(8,128)(2,1)S(1)}) custom-call(bf16[192,5120]{1,0:T(8,128)(2,1)} %ctx_hbm.1, bf16[64,5120]{1,0:T(8,128)(2,1)} %patch_hbm.1, f32[1,5120]{1,0:T(1,128)} %bitcast.17, f32[1,5120]{1,0:T(1,128)} %bitcast.18, ...), custom_call_target="tpu_custom_call" | custom-call | flops 671088640 | bytes 6000000 | tf_op jit(solution)/shard_map/prep/pallas_call | solution.py:297
  30.7 10.5 %all-to-all-done = bf16[256,4,128]{2,1,0:T(4,128)(2,1)S(1)} async-done(((bf16[256,4,128]{2,1,0:T(4,128)(2,1)}), bf16[256,4,128]{2,1,0:T(4,128)(2,1)S(1)}, u32[]{:S(2)}, u32[]{:S(2)}) %all-to-all-start) | async-done | bytes 262176 | tf_op jit(solution)/shard_map/all_to_all | solution.py:295
  41.2 3.1 %embed.1 = bf16[512,5120]{1,0:T(8,128)(2,1)} custom-call(bf16[1024,128]{1,0:T(8,128)(2,1)S(1)} %bitcast.12, bf16[512,256]{1,0:T(8,128)(2,1)S(1)} %get-tuple-element.10.base_ref, bf16[256,5120]{1,0:T(8,128)(2,1)S(1)} %get-tuple-element.11.w_ref, f32[2,5120]{1,0:T(2,128)S(1)} %get-tuple-element.12.vec_ref, bf16[256,512]{1,0:T(8,128)(2,1)S(1)} %get-tuple-element.13.gram_ref, ...), custom_call_target="tpu_custom_call" | custom-call | tf_op jit(solution)/shard_map/embed/pallas_call | solution.py:326
Async XLA Ops:
  4.2 37.0 %all-to-all-start = ((bf16[256,4,128]{2,1,0:T(4,128)(2,1)}), bf16[256,4,128]{2,1,0:T(4,128)(2,1)S(1)}, u32[]{:S(2)}, u32[]{:S(2)}) async-start(bf16[256,4,128]{2,1,0:T(4,128)(2,1)} %bitcast.3), calls=%async_computation | async-start | bytes 524288 | tf_op jit(solution)/shard_map/all_to_all | solution.py:295

commit v6 on v5

--- a/solution.py
+++ b/solution.py
@@ -157,8 +157,8 @@
 
 def prep_kernel(
     ctx_hbm, patch_hbm, pb_hbm, cb_hbm, shift_hbm, scale_hbm, noisy_hbm, mask_hbm, conv_bias_hbm, mwt_hbm, mb_hbm,
-    w_ref, vec_ref, gram_ref, aux_ref, base_ref,
-    ctx_ref, rows_ref, noisy_ref, conv_bias_ref, mwt_ref, mb_ref, sem,
+    w_ref, vec_ref, gram_ref, aux_ref, base_ref, cross_ref,
+    mask_ref, ctx_ref, rows_ref, noisy_ref, conv_bias_ref, mwt_ref, mb_ref, sem,
 ):
     z = mwt_ref.shape[0]
     lat = 4 * z
@@ -175,7 +175,7 @@
             (shift_hbm, rows_ref.at[2]),
             (scale_hbm, rows_ref.at[3]),
             (noisy_hbm, noisy_ref),
-            (mask_hbm, base_ref.at[:, pl.ds(2 * lat, 2 * lat)]),
+            (mask_hbm, mask_ref),
             (conv_bias_hbm, conv_bias_ref),
             (mwt_hbm, mwt_ref),
             (mb_hbm, mb_ref),
@@ -201,27 +201,39 @@
     mean_col = dot_nt(w, ones)[:, :1] / width
     gram = dot_nt(w, w) / width - mean_col * mean_w
     high, low = halves(gram)
-    gram_ref[:, :size] = high
-    gram_ref[:, size:] = low
+    half = 2 * lat
+    inside = (iota((half, half), 0) < lat) & (iota((half, half), 1) < lat)
+    nil = jnp.zeros((half, half), BF)
+    gram_ref[:half] = jnp.where(inside, high[:half, :half], nil)
+    gram_ref[half:] = jnp.where(inside, low[:half, :half], nil)
+    place = (iota((lat, half), 1) == iota((lat, half), 0) + lat).astype(BF)
+    noisy = lax.dot_general(noisy_ref[...], place, (((0,), (0,)), ((), ())), preferred_element_type=F32).astype(BF)
+    base_ref[:, :half] = noisy
+    local = jnp.concatenate([noisy, mask_ref[...]], 1)
+    base_ref[:, half:] = mask_ref[...]
+    linear = 2.0 * (sums[1:2] + sums[2:3]) / width
     square = jnp.mean(centred * centred, axis=1, keepdims=True)
+    tokens = local.shape[0]
+    for r in range(0, tokens, tokens // 2):
+        part = local[r : r + tokens // 2]
+        y = dot(part, high) + dot(part, low)
+        alone = jnp.sum((y + linear) * part.astype(F32), axis=1, keepdims=True) + square
+        lane = iota((1, half), 1)
+        cross_ref[r : r + tokens // 2] = jnp.where(
+            lane < lat, 2.0 * y[:, :half] + linear[:, :half], jnp.where(lane == lat, alone, 0.0)
+        )
     tiled = jnp.concatenate([mwt_ref[...]] * 8, 0)
     conv_bias = jnp.broadcast_to(conv_bias_ref[...], (8, conv_bias_ref.shape[1]))
     latent_bias = lax.dot_general(conv_bias, tiled, NT, precision=lax.Precision.HIGHEST, preferred_element_type=F32)
     latent_bias = latent_bias[:1] + jnp.concatenate([mb_ref[...]] * 8, 1)
-    aux_ref[0:1] = 2.0 * (sums[1:2] + sums[2:3]) / width
-    aux_ref[1:2] = jnp.broadcast_to(square, (1, size))
-    aux_ref[2:3] = jnp.concatenate([latent_bias] * (size // latent_bias.shape[1]), 1)
-    aux_ref[3:8] = jnp.zeros((5, size), F32)
+    aux_ref[...] = jnp.broadcast_to(latent_bias, aux_ref.shape)
     w_ref[...] = ((w.astype(F32) - mean_col) * gain).astype(BF)
-    place = (iota((lat, 2 * lat), 1) == iota((lat, 2 * lat), 0) + lat).astype(BF)
-    noisy = lax.dot_general(noisy_ref[...], place, (((0,), (0,)), ((), ())), preferred_element_type=F32)
-    base_ref[:, : 2 * lat] = noisy.astype(BF)
 
 
 BLOCKS = 10
 
 
-def embed_kernel(arrived_ref, base_ref, w_ref, vec_ref, gram_ref, aux_ref, out_hbm, out_ref, sem):
+def embed_kernel(arrived_ref, base_ref, w_ref, vec_ref, gram_ref, aux_ref, cross_ref, out_hbm, out_ref, sem):
     block = w_ref.shape[1] // BLOCKS
     columns = lambda n: pl.ds(n * block, block)
     tokens = base_ref.shape[0]
@@ -233,17 +245,14 @@
     down = jnp.where(row == 0, 0.0, pltpu.roll(crossed, 1, 0))
     up = jnp.where(row == tokens - 1, 0.0, pltpu.roll(crossed, tokens - 1, 0))
     lane = iota((1, lanes), 1)
-    latent = both + jnp.where(lane // z % 2 == 0, down, up) + aux_ref[2:3, :lanes]
+    latent = both + jnp.where(lane // z % 2 == 0, down, up) + aux_ref[0:1]
     front = jnp.where(lane < lanes // 2, latent, base_ref[:, :lanes].astype(F32))
     x = jnp.concatenate([front.astype(BF), base_ref[:, lanes:]], 1)
-    size = x.shape[1]
-    scales = []
-    for r in range(0, tokens, 256):
-        xr = x[r : r + 256]
-        y = dot(xr, gram_ref[:, :size]) + dot(xr, gram_ref[:, size:])
-        variance = jnp.sum((y + aux_ref[0:1]) * xr.astype(F32), axis=1, keepdims=True) + aux_ref[1:2, :1]
-        scales.append(lax.rsqrt(jnp.maximum(variance, 0.0) + 1e-6))
-    scale = jnp.concatenate(scales, 0)
+    one = jnp.where(lane == lanes // 2, 1.0, 0.0)
+    own = jnp.where(lane < lanes // 2, latent.astype(BF).astype(F32), one)
+    y = dot(jnp.concatenate([own.astype(BF)] * 2, 1), gram_ref[...]) + cross_ref[...]
+    variance = jnp.sum(y * own, axis=1, keepdims=True)
+    scale = lax.rsqrt(jnp.maximum(variance, 0.0) + 1e-6)
     sent = []
     for n in range(BLOCKS):
         at = slice(n * block, (n + 1) * block)
@@ -294,18 +303,20 @@
     )(tile, *in_hbm(section_input, norm_gain, conv_weight.T, mean_weight.T))
     arrived = lax.all_to_all(message.reshape(shards, 4, 8 * z), ("tile", "seq"), 0, 0)
     arrived = arrived.reshape(shards * 4, 8 * z)
-    weights, vectors, gram, aux, base = pl.pallas_call(
+    weights, vectors, gram, aux, base, cross = pl.pallas_call(
         prep_kernel,
         out_shape=(
             jax.ShapeDtypeStruct((features, width), BF),
             jax.ShapeDtypeStruct((2, width), F32),
-            jax.ShapeDtypeStruct((features, 2 * features), BF),
-            jax.ShapeDtypeStruct((8, features), F32),
+            jax.ShapeDtypeStruct((16 * z, 8 * z), BF),
+            jax.ShapeDtypeStruct((8, 8 * z), F32),
             jax.ShapeDtypeStruct((tokens, features), BF),
+            jax.ShapeDtypeStruct((tokens, 8 * z), F32),
         ),
         in_specs=[hbm] * 11,
-        out_specs=(vmem,) * 5,
+        out_specs=(vmem,) * 6,
         scratch_shapes=[
+            pltpu.VMEM(mask_tokens.shape, BF),
             pltpu.VMEM((4 * z, width), BF),
             pltpu.VMEM((4, 1, width), F32),
             pltpu.VMEM(noisy_tokens.shape[::-1], BF),
@@ -326,7 +337,7 @@
     return pl.pallas_call(
         embed_kernel,
         out_shape=jax.ShapeDtypeStruct((tokens, width), BF),
-        in_specs=[vmem] * 6,
+        in_specs=[vmem] * 7,
         out_specs=hbm,
         scratch_shapes=[
             pltpu.VMEM((tokens, width), BF),
@@ -334,7 +345,7 @@
         ],
         compiler_params=params(24),
         name="embed",
-    )(*in_vmem(arrived, base, weights, vectors, gram, aux))
+    )(*in_vmem(arrived, base, weights, vectors, gram, aux, cross))
 
 
 def solution(mesh):

time: 44.6 us -> 44.4 us (level)
  transfers between devices with their start and end apart: 1 -> 1, of which waited for: 1 -> 1; matrix products, arithmetic and copies ran while one was open for 0% -> 0% of each run, Pallas kernels for 11% -> 12%
where the time goes in v6:
time: 44.4 us; the launch traced here: 44.2 us
  starting transfers between devices  21.4 us (48%)
  Pallas kernels  12.5 us (28%)
  waiting for transfers between devices  10.2 us (23%)
    all_to_all x1, starting transfers between devices, body(): lax.all_to_all(message.reshape(shards, 4, 8 * z), ('tile', 'seq'), 0, 0)  21.4 us
    all_to_all x1, waiting for transfers between devices, body(): lax.all_to_all(message.reshape(shards, 4, 8 * z), ('tile', 'seq'), 0, 0)  10.2 us
    pallas_call x1, Pallas kernels, body(): pl.pallas_call(prep_kernel, out_shape=(jax.ShapeDtypeStruct((features, wi...  5.35 us
    pallas_call x1, Pallas kernels, body(): pl.pallas_call(encode_kernel, out_shape=jax.ShapeDtypeStruct((shards * 4,...  4.22 us
    pallas_call x1, Pallas kernels, body(): pl.pallas_call(embed_kernel, out_shape=jax.ShapeDtypeStruct((tokens, widt...  2.9 us
  transfers between devices with their start and end apart: 1, of which 1 were waited for; matrix products, arithmetic and copies ran while one was open for 0% of the time, Pallas kernels for 12%

profile of v6, /device:TPU:8, one launch (start us, length us, event | category | flops | bytes accessed | tf_op | source)
XLA Modules:
  0.0 44.2 jit_solution(4353124428771154986)
XLA Ops:
  0.0 4.2 %encode.1 = bf16[1024,128]{1,0:T(8,128)(2,1)} custom-call(s32[1]{0:T(128)} %bitcast.tile_ref, bf16[2,128,8,384]{3,2,1,0:T(8,128)(2,1)} %x_hbm.1, f32[384]{0:T(512)} %gain_hbm.1, bf16[864,384]{1,0:T(8,128)(2,1)} %bitcast.13, f32[16,32]{1,0:T(8,128)} %bitcast.15), custom_call_target="tpu_custom_call" | custom-call | tf_op jit(solution)/shard_map/encode/pallas_call | solution.py:285
  4.2 21.4 %all-to-all-start = ((bf16[256,4,128]{2,1,0:T(4,128)(2,1)}), bf16[256,4,128]{2,1,0:T(4,128)(2,1)S(1)}, u32[]{:S(2)}, u32[]{:S(2)}) async-start(bf16[256,4,128]{2,1,0:T(4,128)(2,1)} %bitcast.3), calls=%async_computation | async-start | bytes 524288 | tf_op jit(solution)/shard_map/all_to_all | solution.py:304
  25.7 5.3 %prep.1 = (bf16[256,5120]{1,0:T(8,128)(2,1)S(1)}, f32[2,5120]{1,0:T(2,128)S(1)}, bf16[256,128]{1,0:T(8,128)(2,1)S(1)}, f32[8,128]{1,0:T(8,128)S(1)}, bf16[512,25...) custom-call(bf16[192,5120]{1,0:T(8,128)(2,1)} %ctx_hbm.1, bf16[64,5120]{1,0:T(8,128)(2,1)} %patch_hbm.1, f32[1,5120]{1,0:T(1,128)} %bitcast.17, ...), custom_call_target="tpu_custom_call" | custom-call | flops 671088640 | bytes 6000000 | tf_op jit(solution)/shard_map/prep/pallas_call | solution.py:306
  31.0 10.2 %all-to-all-done = bf16[256,4,128]{2,1,0:T(4,128)(2,1)S(1)} async-done(((bf16[256,4,128]{2,1,0:T(4,128)(2,1)}), bf16[256,4,128]{2,1,0:T(4,128)(2,1)S(1)}, u32[]{:S(2)}, u32[]{:S(2)}) %all-to-all-start) | async-done | bytes 262176 | tf_op jit(solution)/shard_map/all_to_all | solution.py:304
  41.2 2.9 %embed.1 = bf16[512,5120]{1,0:T(8,128)(2,1)} custom-call(bf16[1024,128]{1,0:T(8,128)(2,1)S(1)} %bitcast.12, bf16[512,256]{1,0:T(8,128)(2,1)S(1)} %get-tuple-element.11.base_ref, bf16[256,5120]{1,0:T(8,128)(2,1)S(1)} %get-tuple-element.12.w_ref, f32[2,5120]{1,0:T(2,128)S(1)} %get-tuple-element.13.vec_ref, bf16[256,128]{1,0:T(8,128)(2,1)S(1)} %get-tuple-element.14.gram_ref, ...), custom_call_target="tpu_custom_call" | custom-call | tf_op jit(solution)/shard_map/embed/pallas_call | solution.py:337
Async XLA Ops:
  4.2 37.0 %all-to-all-start = ((bf16[256,4,128]{2,1,0:T(4,128)(2,1)}), bf16[256,4,128]{2,1,0:T(4,128)(2,1)S(1)}, u32[]{:S(2)}, u32[]{:S(2)}) async-start(bf16[256,4,128]{2,1,0:T(4,128)(2,1)} %bitcast.3), calls=%async_computation | async-start | bytes 524288 | tf_op jit(solution)/shard_map/all_to_all | solution.py:304

commit v7 on v6

--- a/solution.py
+++ b/solution.py
@@ -127,9 +127,9 @@
                 jnp.where(first, ext[3], ext[1]),
             )
             for f in range(4):
-                at = ((p * 4 + f) * (pairs // 2) + c * CHUNK // 2) * columns
-                size = CHUNK // 2 * columns
-                parts[at : at + size] = slots[f].reshape(size, lanes)
+                for m in range(CHUNK // 2):
+                    at = (f * pairs + c * CHUNK + 2 * m + p) * columns
+                    parts[at : at + columns] = slots[f][m]
 
     done = 0
     for j in range(blocks):
@@ -239,7 +239,8 @@
     tokens = base_ref.shape[0]
     lanes = arrived_ref.shape[1]
     z = lanes // 8
-    both = arrived_ref[:tokens].astype(F32) + arrived_ref[tokens:].astype(F32)
+    arrived = arrived_ref[...].astype(F32).reshape(tokens // 4, 8, lanes)
+    both = (arrived[:, :4] + arrived[:, 4:]).reshape(tokens, lanes)
     crossed = pltpu.roll(both, lanes // 2, 1)
     row = iota((tokens, 1), 0)
     down = jnp.where(row == 0, 0.0, pltpu.roll(crossed, 1, 0))
@@ -301,7 +302,7 @@
         compiler_params=params(24),
         name="encode",
     )(tile, *in_hbm(section_input, norm_gain, conv_weight.T, mean_weight.T))
-    arrived = lax.all_to_all(message.reshape(shards, 4, 8 * z), ("tile", "seq"), 0, 0)
+    arrived = lax.all_to_all(message.reshape(shards, 4, 8 * z), ("seq", "tile"), 0, 0)
     arrived = arrived.reshape(shards * 4, 8 * z)
     weights, vectors, gram, aux, base, cross = pl.pallas_call(
         prep_kernel,

time: 44.4 us -> 43.9 us (0.989)
  the two profiles are of different devices: /device:TPU:8 before, /device:TPU:16 now
where the time goes in v7:
time: 43.9 us; the launch traced here: 43.7 us
  starting transfers between devices  22 us (50%)
  Pallas kernels  12.5 us (28%)
  waiting for transfers between devices  9.14 us (21%)
    all_to_all x1, starting transfers between devices, body(): lax.all_to_all(message.reshape(shards, 4, 8 * z), ('seq', 'tile'), 0, 0)  22 us
    all_to_all x1, waiting for transfers between devices, body(): lax.all_to_all(message.reshape(shards, 4, 8 * z), ('seq', 'tile'), 0, 0)  9.14 us
    pallas_call x1, Pallas kernels, body(): pl.pallas_call(prep_kernel, out_shape=(jax.ShapeDtypeStruct((features, wi...  5.34 us
    pallas_call x1, Pallas kernels, body(): pl.pallas_call(encode_kernel, out_shape=jax.ShapeDtypeStruct((shards * 4,...  4.25 us
    pallas_call x1, Pallas kernels, body(): pl.pallas_call(embed_kernel, out_shape=jax.ShapeDtypeStruct((tokens, widt...  2.93 us
  transfers between devices with their start and end apart: 1, of which 1 were waited for; matrix products, arithmetic and copies ran while one was open for 0% of the time, Pallas kernels for 12%

profile of v7, /device:TPU:16, one launch (start us, length us, event | category | flops | bytes accessed | tf_op | source)
XLA Modules:
  0.0 43.7 jit_solution(5942590815592139003)
XLA Ops:
  0.0 4.2 %encode.1 = bf16[1024,128]{1,0:T(8,128)(2,1)} custom-call(s32[1]{0:T(128)} %bitcast.tile_ref, bf16[2,128,8,384]{3,2,1,0:T(8,128)(2,1)} %x_hbm.1, f32[384]{0:T(512)} %gain_hbm.1, bf16[864,384]{1,0:T(8,128)(2,1)} %bitcast.13, f32[16,32]{1,0:T(8,128)} %bitcast.15), custom_call_target="tpu_custom_call" | custom-call | tf_op jit(solution)/shard_map/encode/pallas_call | solution.py:286
  4.3 22.0 %all-to-all-start = ((bf16[256,4,128]{2,1,0:T(4,128)(2,1)}), bf16[256,4,128]{2,1,0:T(4,128)(2,1)S(1)}, u32[]{:S(2)}, u32[]{:S(2)}) async-start(bf16[256,4,128]{2,1,0:T(4,128)(2,1)} %bitcast.3), calls=%async_computation | async-start | bytes 524288 | tf_op jit(solution)/shard_map/all_to_all | solution.py:305
  26.3 5.3 %prep.1 = (bf16[256,5120]{1,0:T(8,128)(2,1)S(1)}, f32[2,5120]{1,0:T(2,128)S(1)}, bf16[256,128]{1,0:T(8,128)(2,1)S(1)}, f32[8,128]{1,0:T(8,128)S(1)}, bf16[512,25...) custom-call(bf16[192,5120]{1,0:T(8,128)(2,1)} %ctx_hbm.1, bf16[64,5120]{1,0:T(8,128)(2,1)} %patch_hbm.1, f32[1,5120]{1,0:T(1,128)} %bitcast.17, ...), custom_call_target="tpu_custom_call" | custom-call | flops 671088640 | bytes 6000000 | tf_op jit(solution)/shard_map/prep/pallas_call | solution.py:307
  31.6 9.1 %all-to-all-done = bf16[256,4,128]{2,1,0:T(4,128)(2,1)S(1)} async-done(((bf16[256,4,128]{2,1,0:T(4,128)(2,1)}), bf16[256,4,128]{2,1,0:T(4,128)(2,1)S(1)}, u32[]{:S(2)}, u32[]{:S(2)}) %all-to-all-start) | async-done | bytes 262176 | tf_op jit(solution)/shard_map/all_to_all | solution.py:305
  40.7 2.9 %embed.1 = bf16[512,5120]{1,0:T(8,128)(2,1)} custom-call(bf16[1024,128]{1,0:T(8,128)(2,1)S(1)} %bitcast.12, bf16[512,256]{1,0:T(8,128)(2,1)S(1)} %get-tuple-element.11.base_ref, bf16[256,5120]{1,0:T(8,128)(2,1)S(1)} %get-tuple-element.12.w_ref, f32[2,5120]{1,0:T(2,128)S(1)} %get-tuple-element.13.vec_ref, bf16[256,128]{1,0:T(8,128)(2,1)S(1)} %get-tuple-element.14.gram_ref, ...), custom_call_target="tpu_custom_call" | custom-call | tf_op jit(solution)/shard_map/embed/pallas_call | solution.py:338
Async XLA Ops:
  4.3 36.5 %all-to-all-start = ((bf16[256,4,128]{2,1,0:T(4,128)(2,1)}), bf16[256,4,128]{2,1,0:T(4,128)(2,1)S(1)}, u32[]{:S(2)}, u32[]{:S(2)}) async-start(bf16[256,4,128]{2,1,0:T(4,128)(2,1)} %bitcast.3), calls=%async_computation | async-start | bytes 524288 | tf_op jit(solution)/shard_map/all_to_all | solution.py:305
